TPU v7x, 128 devices: a whole 4x4x4 slice. The times are simulated.
128 devices in a mesh: slab: 16 (over x, y), group: 8 (over z, core).
Axes of the slice: x: 4, y: 4, z: 4, core: 2. Of those that a mesh axis runs over, the one named last changes fastest.
Arguments:
- disp_now: float32 [3, 524288], P(None, 'slab'), may hold values from -6 to 6
- disp_prev: float32 [3, 524288], P(None, 'slab'), may hold values from -6 to 6
- inv_mass: float32 [524288], P('slab'), may hold values from 0.5 to 2
- cell_nodes: int32 [4096, 192], P(('slab', 'group')), may hold values from 0 to 98303
- shape_grads: bfloat16 [4096, 3, 192, 128], P(('slab', 'group')), may hold values from -0.125 to 0.125
- cell_weights: float32 [4096, 128], P(('slab', 'group')), may hold values from 0.5 to 2
- cell_shear: float32 [4096], P(('slab', 'group')), may hold values from 0.5 to 2
- cell_bulk: float32 [4096], P(('slab', 'group')), may hold values from 1 to 4
- block_owner: int32 [4096, 1], P(('slab', 'group')), may hold values from 0 to 15; in each aligned block of 32 rows (0 to 31, 32 to 63, ...) at most 4 rows name the same one
- block_nodes: int32 [4096, 256], P(('slab', 'group')), may hold values from 0 to 32767
- block_phi: float32 [4096, 128, 256], P(('slab', 'group')), may hold values from -0.375 to 0.375
- block_corr: float32 [4096, 128, 128], P(('slab', 'group')), may hold values from -0.5 to 0.5
- block_target: float32 [4096, 3, 128], P(('slab', 'group')), may hold values from -6 to 6
- block_fixed: int32 [4096, 128], P(('slab', 'group')), may hold values 0 or 1
Outputs:
- disp_final: float32 [3, 524288], P(None, 'slab')
Inputs may be any that keep to these rules, and one draw needn't show every extreme that they name: `cell_nodes`: support node numbers run over the slab below, the cell's own slab and the slab above; those outside the head read zero. `block_owner`: among the 32 blocks of one device at most 4 have one owner slab, and in every draw some device has exactly 4 with one owner.
All inputs are finite; a program needn't handle non-finite values. No bound on the sum of `block_fixed` on one device may be relied on, other than what follows from the above.
Results may differ from a plain program's by a relative error of at most 0.0059.
Values may be sent and summed in bfloat16 or wider, within the bound.
A program may use at most 192 MiB of HBM per device.

v0:
```python
import jax
import jax.numpy as jnp
from jax import lax
from jax.sharding import PartitionSpec as P

CAP = 4


def extended(block, sides, width):
    for axis, dim in sides:
        count = lax.axis_size(axis)
        forward = [(i, i + 1) for i in range(count - 1)]
        backward = [(target, source) for source, target in forward]
        low = lax.ppermute(
            lax.slice_in_dim(block, block.shape[dim] - width, None, axis=dim), axis, forward
        )
        high = lax.ppermute(lax.slice_in_dim(block, 0, width, axis=dim), axis, backward)
        block = jnp.concatenate([low, block, high], axis=dim)
    return block


def from_behind(array, axis, by):
    size = lax.axis_size(axis)
    pairs = [(i, i + by) for i in range(size) if 0 <= i + by < size]
    return lax.ppermute(array, axis, pairs)


def stress_of(grad, shear, bulk):
    identity = jnp.eye(3, dtype=grad.dtype)
    full = grad + identity[None, :, :, None]
    entries = [[full[:, leading, trailing] for trailing in range(3)] for leading in range(3)]
    cofactor = [
        [
            entries[(leading + 1) % 3][(trailing + 1) % 3]
            * entries[(leading + 2) % 3][(trailing + 2) % 3]
            - entries[(leading + 1) % 3][(trailing + 2) % 3]
            * entries[(leading + 2) % 3][(trailing + 1) % 3]
            for trailing in range(3)
        ]
        for leading in range(3)
    ]
    volume = (
        entries[0][0] * cofactor[0][0]
        + entries[0][1] * cofactor[0][1]
        + entries[0][2] * cofactor[0][2]
    )
    clamped = jnp.maximum(volume, 0.3)
    shear_now = shear[:, None]
    factor = (bulk[:, None] * jnp.log(clamped) - shear_now) / clamped
    rows_out = [
        jnp.stack(
            [
                shear_now * entries[leading][trailing] + factor * cofactor[leading][trailing]
                for trailing in range(3)
            ],
            axis=1,
        )
        for leading in range(3)
    ]
    return jnp.stack(rows_out, axis=1)


def body(
    disp_now,
    disp_prev,
    inv_mass,
    cell_nodes,
    shape_grads,
    cell_weights,
    cell_shear,
    cell_bulk,
    block_owner,
    block_nodes,
    block_phi,
    block_corr,
    block_target,
    block_fixed,
):
    width = disp_now.shape[1]
    slabs = lax.axis_size("slab")
    nearby = extended(disp_now.astype(jnp.bfloat16), (("slab", 1),), width)
    gathered = jnp.moveaxis(jnp.take(nearby, cell_nodes, axis=1), 0, 1)
    grad = jnp.einsum("cia,cjap->cijp", gathered, shape_grads, preferred_element_type=jnp.float32)
    stress = stress_of(grad, cell_shear, cell_bulk)
    weighted = (cell_weights[:, None, None, :] * stress).astype(jnp.bfloat16)
    force = jnp.einsum("cijp,cjap->cia", weighted, shape_grads, preferred_element_type=jnp.float32)
    partial_value = (
        jnp.zeros((3, 3 * width), jnp.float32).at[:, cell_nodes].add(jnp.moveaxis(force, 1, 0))
    )
    summed = lax.psum(partial_value, "group")
    from_above = from_behind(summed[:, :width], "slab", -1)
    from_below = from_behind(summed[:, 2 * width :], "slab", 1)
    force_sum = summed[:, width : 2 * width] + from_above + from_below
    disp_next = 2.0 * disp_now - disp_prev - inv_mass[None, :] * force_sum
    support = block_nodes.shape[1]
    owner = block_owner[:, 0]
    matches = (owner[:, None] == jnp.arange(slabs, dtype=jnp.int32)[None, :]).astype(jnp.int32)
    ranked = jnp.sum((jnp.cumsum(matches, axis=0) - matches) * matches, axis=1)
    slot_of = owner * CAP + ranked
    fixed_mask = block_fixed.astype(jnp.float32)
    highest = lax.Precision.HIGHEST
    request = jnp.zeros((slabs * CAP, support), jnp.int32).at[slot_of].set(block_nodes)
    request = request.reshape(slabs, CAP, support)
    asked = lax.all_to_all(request, "slab", split_axis=0, concat_axis=0, tiled=True)
    looked = jnp.moveaxis(jnp.take(disp_next, asked, axis=1), 0, 2)
    returned = lax.all_to_all(looked, "slab", split_axis=0, concat_axis=0, tiled=True)
    returned, asked = (returned, asked)
    values = returned.reshape(slabs * CAP, 3, support)[slot_of]
    interp = jnp.einsum("bma,bia->bim", block_phi, values, precision=highest)
    resid = fixed_mask[:, None, :] * (block_target - interp)
    corr = jnp.einsum("bmq,biq->bim", block_corr, resid, precision=highest)
    delta = jnp.einsum("bma,bim->bia", block_phi, corr, precision=highest)
    outgoing = jnp.zeros((slabs * CAP, 3, support), jnp.float32).at[slot_of].set(delta)
    arrived = lax.all_to_all(
        outgoing.reshape(slabs, CAP, 3, support), "slab", split_axis=0, concat_axis=0, tiled=True
    )
    added = jnp.zeros((3, width), jnp.float32).at[:, asked].add(jnp.moveaxis(arrived, 2, 0))
    return disp_next + lax.psum(added, "group")


def solution(mesh):
    placed = (
        P(None, "slab"),
        P(None, "slab"),
        P("slab"),
        P(("slab", "group"), None),
        P(("slab", "group"), None, None, None),
        P(("slab", "group"), None),
        P(("slab", "group")),
        P(("slab", "group")),
        P(("slab", "group"), None),
        P(("slab", "group"), None),
        P(("slab", "group"), None, None),
        P(("slab", "group"), None, None),
        P(("slab", "group"), None, None),
        P(("slab", "group"), None),
    )
    return jax.shard_map(
        body, mesh=mesh, in_specs=placed, out_specs=P(None, "slab"), check_vma=False
    )
```

profile of v0, /device:TPU:1, one launch (start us, length us, event | category | flops | bytes accessed | tf_op | source)
XLA Modules:
  0.0 561.9 jit_solution(1684865080098660417)
XLA Ops:
  6.5 1.3 convert_element_type.19
  7.8 4.0 collective-permute-start
  11.9 1.3 collective-permute-start.1
  13.2 0.8 compare_select_fusion.1
  14.0 0.1 reshape.1417
  14.0 0.7 fusion.18
  14.8 0.8 select_reduce_fusion
  15.7 0.8 compare_and_fusion.1
  16.4 0.4 collective-permute-done
  16.8 3.9 collective-permute-done.1
  20.7 1.3 pad_maximum_fusion
  22.0 15.8 %copy.131 = bf16[3,98304]{0,1:T(8,128)(2,1)} copy(bf16[3,98304]{1,0:T(4,128)(2,1)S(1)} %pad_maximum_fusion) | data formatting | bytes 1179648 | tf_op jit(solution)/shard_map/concatenate | solution.py:18
  37.8 32.5 %gather_fusion = bf16[6144,3]{1,0:T(8,128)(2,1)} fusion(bf16[3,98304]{0,1:T(8,128)(2,1)} %copy.131, s32[6144]{0:T(1024)S(1)} %broadcast_clamp_fusion.1), kind=kCustom, calls=%fused_computation | custom fusion | bytes 98304 | tf_op jit(solution)/shard_map/jit(_take)/gather | solution.py:82
  70.4 1.9 copy.132
  72.3 3.3 fusion.10
  75.6 0.1 copy_add_fusion
  75.7 0.1 multiply_add_fusion.8
  75.7 0.1 multiply_add_fusion.7
  76.0 4.1 convolution_bitcast_fusion
  80.0 2.2 copy.149
  82.2 53.3 %scatter_custom_fusion = f32[3,98304]{0,1:T(8,128)} fusion(s32[6144]{0:T(1024)S(1)} %reshape.1417, f32[6144,3]{1,0:T(8,128)} %bitcast.170, f32[]{:T(128)} %constant.16.clone.1), kind=kCustom, calls=%fused_computation.7 | custom fusion | flops 18432 | bytes 1180160 | tf_op jit(solution)/shard_map/scatter-add | solution.py:88
  135.5 26.7 %copy.137 = f32[3,98304]{1,0:T(4,128)} copy(f32[3,98304]{0,1:T(8,128)} %scatter_custom_fusion) | data formatting | bytes 2359296 | tf_op jit(solution)/shard_map/scatter-add | solution.py:88
  162.3 1.0 scatter_custom_fusion.1
  163.3 14.3 %all_to_all.15 = s32[16,4,256]{2,1,0:T(4,128)S(1)} all-to-all(s32[16,4,256]{2,1,0:T(4,128)S(1)} %reshape.1388), channel_id=1, replica_groups=mesh['slab'=16,'group'=8] {'slab'}, dimensions={0} | all-to-all | bytes 131072 | tf_op jit(solution)/shard_map/all_to_all | solution.py:104
  177.7 51.8 %all-reduce.3.cloned.1.call-done = f32[3,98304]{1,0:T(4,128)} async-done(((f32[3,98304]{1,0:T(4,128)}), f32[3,98304]{1,0:T(4,128)}) %all-reduce.3.cloned.1.call-update) | async-done | bytes 1179664 | tf_op jit(solution)/shard_map/psum | solution.py:90
  229.5 1.4 fusion.22
  230.9 1.3 collective-permute-start.2
  232.2 4.0 collective-permute-start.3
  236.2 7.3 %collective-permute-done.2 = f32[3,32768]{1,0:T(4,128)S(1)} collective-permute-done((f32[3,32768]{1,0:T(4,128)S(1)}, f32[3,32768]{1,0:T(4,128)S(1)}, u32[]{:S(2)}, u32[]{:S(2)}) %collective-permute-start.2) | collective-permute-done | bytes 393248 | tf_op jit(solution)/shard_map/ppermute | solution.py:25
  243.5 0.9 collective-permute-done.3
  244.5 1.6 fusion.7
  246.0 8.6 %copy.138 = f32[3,32768]{0,1:T(8,128)} copy(f32[3,32768]{1,0:T(4,128)S(1)} %fusion.7) | data formatting | bytes 786432 | tf_op jit(solution)/shard_map/sub | solution.py:94
  254.6 60.3 %gather_fusion.1 = f32[16384,3]{1,0:T(8,128)} fusion(f32[3,32768]{0,1:T(8,128)} %copy.138, s32[16384]{0:T(1024)S(1)} %broadcast_clamp_fusion), kind=kCustom, calls=%fused_computation.1 | custom fusion | bytes 458752 | tf_op jit(solution)/shard_map/jit(_take)/gather | solution.py:105
  314.9 5.2 copy.139
  320.1 0.7 select_bitcast_fusion
  320.9 9.4 %all-to-all-start.1 = ((f32[16,4,3,256]{3,1,2,0:T(4,128)}), f32[16,4,3,256]{3,1,2,0:T(4,128)S(1)}, u32[]{:S(2)}, u32[]{:S(2)}) async-start(f32[16,4,3,256]{3,1,2,0:T(4,128)} %select_bitcast_fusion), calls=%async_computation.1 | async-start | bytes 393216 | tf_op jit(solution)/shard_map/all_to_all | solution.py:106
  330.3 6.8 %all-to-all-done.1 = f32[16,4,3,256]{3,1,2,0:T(4,128)S(1)} async-done(((f32[16,4,3,256]{3,1,2,0:T(4,128)}), f32[16,4,3,256]{3,1,2,0:T(4,128)S(1)}, u32[]{:S(2)}, u32[]{:S(2)}) %all-to-all-start.1) | async-done | bytes 196640 | tf_op jit(solution)/shard_map/all_to_all | solution.py:106
  337.2 0.6 gather_fusion.2
  337.9 5.8 %fusion.4 = f32[32,3,128]{2,1,0:T(4,128)S(1)} fusion(f32[32,3,256]{2,1,0:T(4,128)S(1)} %gather_fusion.2, f32[32,128,256]{2,1,0:T(8,128)} %param.24, f32[32,3,128]{2,0,1:T(8,128)S(1)} %copy-done.4, f32[32,128]{1,0:T(8,128)S(1)} %convert_element_type.23), kind=kOutput, calls=%fused_computation.13 | convolution fusion | flops 37773312 | bytes 4407296 | tf_op jit(solution)/shard_map/bma,bia->bim/dot_general | solution.py:109
  343.7 3.4 fusion.23
  347.1 2.1 fusion.24
  349.3 1.5 scatter_fusion
  350.8 10.2 %all_to_all.16 = f32[16,4,3,256]{3,1,2,0:T(4,128)S(1)} all-to-all(f32[16,4,3,256]{3,1,2,0:T(4,128)S(1)} %copy.143), channel_id=1, replica_groups=mesh['slab'=16,'group'=8] {'slab'}, dimensions={0} | all-to-all | bytes 393216 | tf_op jit(solution)/shard_map/all_to_all | solution.py:114
  361.0 4.6 copy.151
  365.6 106.9 %scatter_custom_fusion.3 = f32[3,32768]{0,1:T(8,128)} fusion(s32[16384]{0:T(1024)S(1)} %bitcast.176, f32[16384,3]{1,0:T(8,128)} %bitcast.169, f32[]{:T(128)} %constant.16.clone.1), kind=kCustom, calls=%fused_computation.9 | custom fusion | flops 49152 | bytes 393728 | tf_op jit(solution)/shard_map/scatter-add | solution.py:117
  472.5 9.8 %copy.146 = f32[3,32768]{1,0:T(4,128)} copy(f32[3,32768]{0,1:T(8,128)} %scatter_custom_fusion.3) | data formatting | bytes 786432 | tf_op jit(solution)/shard_map/scatter-add | solution.py:117
  482.4 70.7 %all-reduce.5.cloned.1.call-done = f32[3,32768]{1,0:T(4,128)} async-done(((f32[3,32768]{1,0:T(4,128)}), f32[3,32768]{1,0:T(4,128)}) %all-reduce.5.cloned.1.call-update) | async-done | bytes 393232 | tf_op jit(solution)/shard_map/psum | solution.py:118
  553.1 2.0 add.250
  (42 shorter events, 0.6 us)
Async XLA Ops:
  6.5 337.2 %copy-start = (f32[32,128,128]{2,1,0:T(8,128)S(1)}, f32[32,128,128]{2,1,0:T(8,128)}, u32[]{:S(2)}) copy-start(f32[32,128,128]{2,1,0:T(8,128)} %param.25) | copy-start | bytes 6291460
  6.5 223.0 %all-reduce.3.cloned.1.call-start = ((), (), s32[]{:S(2)}) async-start(), calls=%async_computation.3 | async-start | bytes 3145728 | tf_op jit(solution)/shard_map/psum | solution.py:90
  7.8 9.0 %collective-permute-start = (bf16[3,32768]{1,0:T(4,128)(2,1)S(1)}, bf16[3,32768]{1,0:T(4,128)(2,1)S(1)}, u32[]{:S(2)}, u32[]{:S(2)}) collective-permute-start(bf16[3,32768]{1,0:T(4,128)(2,1)S(1)} %convert_element_type.19), channel_id=1, source_target_pairs={{0,8},{8,16},{16,24},{24,32},{32,40},{40,48},{48,56},{56,64},{64,7... | collective-permute-start | bytes 589832 | tf_op jit(solution)/shard_map/ppermute | solution.py:14
  11.9 8.9 %collective-permute-start.1 = (bf16[3,32768]{1,0:T(4,128)(2,1)S(1)}, bf16[3,32768]{1,0:T(4,128)(2,1)}, u32[]{:S(2)}, u32[]{:S(2)}) collective-permute-start(bf16[3,32768]{1,0:T(4,128)(2,1)S(1)} %convert_element_type.19), channel_id=1, source_target_pairs={{8,0},{16,8},{24,16},{32,24},{40,32},{48,40},{56,48},{64,56},{72,6... | collective-permute-start | bytes 589832 | tf_op jit(solution)/shard_map/ppermute | solution.py:17
  37.8 37.8 %copy-start.7 = (f32[32]{0:T(128)S(1)}, f32[32]{0:T(128)}, u32[]{:S(2)}) copy-start(f32[32]{0:T(128)} %param.20) | copy-start | bytes 388
  37.8 37.8 %copy-start.9 = (f32[32]{0:T(128)S(1)}, f32[32]{0:T(128)}, u32[]{:S(2)}) copy-start(f32[32]{0:T(128)} %param.21) | copy-start | bytes 388
  37.8 38.1 %copy-start.6 = (f32[32,128]{1,0:T(8,128)S(1)}, f32[32,128]{1,0:T(8,128)}, u32[]{:S(2)}) copy-start(f32[32,128]{1,0:T(8,128)} %param.19) | copy-start | bytes 49156
  135.5 26.7 %copy-start.8 = (s32[32,1]{0,1:T(1,128)S(1)}, s32[32,1]{0,1:T(1,128)}, u32[]{:S(2)}) copy-start(s32[32,1]{0,1:T(1,128)} %param.22) | copy-start | bytes 388
  135.5 109.0 %copy-start.3 = (f32[32768]{0:T(1024)S(1)}, f32[32768]{0:T(1024)}, u32[]{:S(2)}) copy-start(f32[32768]{0:T(1024)} %param.16) | copy-start | bytes 393220
  162.2 82.2 %copy-start.2 = (f32[3,32768]{1,0:T(4,128)S(1)}, f32[3,32768]{1,0:T(4,128)}, u32[]{:S(2)}) copy-start(f32[3,32768]{1,0:T(4,128)} %param.14) | copy-start | bytes 1179652
  230.9 12.6 %collective-permute-start.2 = (f32[3,32768]{1,0:T(4,128)S(1)}, f32[3,32768]{1,0:T(4,128)S(1)}, u32[]{:S(2)}, u32[]{:S(2)}) collective-permute-start(f32[3,32768]{1,0:T(4,128)S(1)} %get-tuple-element.9), channel_id=1, source_target_pairs={{8,0},{16,8},{24,16},{32,24},{40,32},{48,40},{56,48},{64,56},{72,6... | collective-permute-start | bytes 1179656 | tf_op jit(solution)/shard_map/ppermute | solution.py:25
  232.2 12.2 %collective-permute-start.3 = (f32[3,32768]{1,0:T(4,128)S(1)}, f32[3,32768]{1,0:T(4,128)S(1)}, u32[]{:S(2)}, u32[]{:S(2)}) collective-permute-start(f32[3,32768]{1,0:T(4,128)S(1)} %get-tuple-element.10), channel_id=1, source_target_pairs={{0,8},{8,16},{16,24},{24,32},{32,40},{40,48},{48,56},{56,64},{64,7... | collective-permute-start | bytes 1179656 | tf_op jit(solution)/shard_map/ppermute | solution.py:25
  314.9 15.4 %copy-start.5 = (s32[32,128]{1,0:T(8,128)S(1)}, s32[32,128]{1,0:T(8,128)}, u32[]{:S(2)}) copy-start(s32[32,128]{1,0:T(8,128)} %param.27) | copy-start | bytes 49156
  314.9 23.0 %copy-start.4 = (f32[32,3,128]{2,0,1:T(8,128)S(1)}, f32[32,3,128]{2,0,1:T(8,128)}, u32[]{:S(2)}) copy-start(f32[32,3,128]{2,0,1:T(8,128)} %param.26) | copy-start | bytes 147460
  320.9 16.3 %all-to-all-start.1 = ((f32[16,4,3,256]{3,1,2,0:T(4,128)}), f32[16,4,3,256]{3,1,2,0:T(4,128)S(1)}, u32[]{:S(2)}, u32[]{:S(2)}) async-start(f32[16,4,3,256]{3,1,2,0:T(4,128)} %select_bitcast_fusion), calls=%async_computation.1 | async-start | bytes 393216 | tf_op jit(solution)/shard_map/all_to_all | solution.py:106
  330.2 222.9 %all-reduce.5.cloned.1.call-start = ((), (), s32[]{:S(2)}) async-start(), calls=%async_computation.4 | async-start | bytes 1048576 | tf_op jit(solution)/shard_map/psum | solution.py:118
  337.9 9.2 %copy-start.1 = (f32[32,128,256]{2,1,0:T(8,128)S(1)}, f32[32,128,256]{2,1,0:T(8,128)}, u32[]{:S(2)}) copy-start(f32[32,128,256]{2,1,0:T(8,128)} %param.24) | copy-start | bytes 12582916
Sparse Core Ops, SparseCore 0:
  162.4 67.1 all-reduce.2
  482.5 70.5 all-reduce.4
where the time goes:
time: 564 us; the launch traced here: 562 us
  local copies, waits for them, and re-layouts  173 us (31%)
  other arithmetic  171 us (30%)
  waiting for transfers between devices  142 us (25%)
  blocking collectives  24.4 us (4%)
  starting transfers between devices  20.1 us (4%)
  matrix products  18.6 us (3%)
  between operations  13.7 us (2%)
    scatter-add x1, other arithmetic, body(): jnp.zeros((3, width), jnp.float32).at[:, asked]  107 us
    psum x1, waiting for transfers between devices, body(): return disp_next + lax.psum(added, 'group')  70.7 us
    gather x2, local copies, waits for them, and re-layouts, body(): looked = jnp.moveaxis(jnp.take(disp_next, asked, axis=1), 0, 2)  65.5 us
    scatter-add x1, other arithmetic, body(): jnp.zeros((3, 3 * width), jnp.float32).at[:, cell_nodes]  53.3 us
    psum x1, waiting for transfers between devices, body(): summed = lax.psum(partial_value, 'group')  51.8 us
    gather x2, local copies, waits for them, and re-layouts, body(): gathered = jnp.moveaxis(jnp.take(nearby, cell_nodes, axis=1), 0, 1)  34.5 us
    scatter-add x1, local copies, waits for them, and re-layouts, body(): jnp.zeros((3, 3 * width), jnp.float32).at[:, cell_nodes]  26.7 us
    concatenate x1, local copies, waits for them, and re-layouts, extended(): block = jnp.concatenate([low, block, high], axis=dim)  15.8 us
  transfers between devices with their start and end apart: 7, of which 7 were waited for; matrix products, arithmetic and copies ran while one was open for 1% of the time, Pallas kernels for 0%

commit v1 on v0

v1 whole, which is shorter than its diff:
```python
import jax
import jax.numpy as jnp
from jax import lax
from jax.experimental import pallas as pl
from jax.experimental.pallas import tpu as pltpu
from jax.sharding import PartitionSpec as P

BF = jnp.bfloat16
F32 = jnp.float32
NT = (((1,), (1,)), ((), ()))
MESH = pl.DeviceIdType.MESH
CAP = 4
QUAD = 768


def onehot(index, size):
    rows = lax.broadcasted_iota(jnp.int32, (size, index.shape[1]), 0)
    return jnp.where(rows == index, 1.0, 0.0).astype(BF)


def cells_kernel(nodes, table, weights, shear, bulk, grads_hbm, out, grads, field, near, columns, spread, sem):
    load = pltpu.make_async_copy(grads_hbm, grads, sem)
    load.start()
    rows_of = lax.broadcasted_iota(jnp.int32, (128, QUAD), 0)

    def gather(quad, carry):
        node = nodes[quad]
        slab, row, column = node >> 15, (node >> 8) & 127, node & 255
        total = None
        for side in range(3):
            hot = onehot(jnp.where(slab == side, column, -1), 256)
            columns[quad, side] = hot
            part = jnp.dot(table[side], hot, preferred_element_type=F32)
            total = part if total is None else total + part
        mask = rows_of == row
        for i in range(3):
            near[quad, i : i + 1, :] = jnp.sum(
                jnp.where(mask, total[128 * i : 128 * i + 128], 0.0), axis=0, keepdims=True
            )
        return carry

    lax.fori_loop(0, 8, gather, 0)
    load.wait()
    sub = lax.broadcasted_iota(jnp.int32, (8, 384), 0)
    lane = lax.broadcasted_iota(jnp.int32, (8, 384), 1)
    own = (sub >= 4) == (lane >= 192)

    def gradient(quad, carry):
        for pair in range(2):
            left = jnp.zeros((8, 384), F32)
            for i in range(3):
                left = jnp.where(sub % 4 == i, near[quad, i : i + 1, 384 * pair : 384 * pair + 384], left)
            left = jnp.where(own, left, 0.0).astype(BF)
            for j in range(3):
                first = 4 * quad + 2 * pair
                both = jnp.concatenate([grads[first, j], grads[first + 1, j]], axis=0)
                at = pl.ds(pl.multiple_of(16 * quad + 8 * pair, 8), 8)
                field[j, at, :] = jnp.dot(left, both, preferred_element_type=F32)
        return carry

    lax.fori_loop(0, 8, gradient, 0)
    full = [
        [field[j, pl.ds(i, 32, stride=4), :] + (1.0 if i == j else 0.0) for j in range(3)]
        for i in range(3)
    ]
    cofactor = [
        [
            full[(i + 1) % 3][(j + 1) % 3] * full[(i + 2) % 3][(j + 2) % 3]
            - full[(i + 1) % 3][(j + 2) % 3] * full[(i + 2) % 3][(j + 1) % 3]
            for j in range(3)
        ]
        for i in range(3)
    ]
    volume = full[0][0] * cofactor[0][0] + full[0][1] * cofactor[0][1] + full[0][2] * cofactor[0][2]
    clamped = jnp.maximum(volume, 0.3)
    mu, weight = shear[...], weights[...]
    factor = (bulk[...] * jnp.log(clamped) - mu) / clamped
    for i in range(3):
        for j in range(3):
            field[j, pl.ds(i, 32, stride=4), :] = weight * (mu * full[i][j] + factor * cofactor[i][j])
    low_lane = lax.broadcasted_iota(jnp.int32, (1, 384), 1) < 192
    rows_pair = lax.broadcasted_iota(jnp.int32, (128, 384), 0)

    def forces(quad, carry):
        for pair in range(2):
            total = None
            for j in range(3):
                first = 4 * quad + 2 * pair
                at = pl.ds(pl.multiple_of(16 * quad + 8 * pair, 8), 8)
                both = jnp.concatenate([grads[first, j], grads[first + 1, j]], axis=0)
                part = lax.dot_general(field[j, at, :].astype(BF), both, NT, preferred_element_type=F32)
                total = part if total is None else total + part
            span = slice(384 * pair, 384 * pair + 384)
            mask = rows_pair == ((nodes[quad, :, span] >> 8) & 127)
            for i in range(3):
                value = jnp.where(low_lane, total[i : i + 1], total[4 + i : 5 + i])
                spread[quad, 128 * i : 128 * i + 128, span] = jnp.where(mask, value, 0.0).astype(BF)
        return carry

    lax.fori_loop(0, 8, forces, 0)
    for side in range(3):
        total = None
        for quad in range(8):
            part = lax.dot_general(spread[quad], columns[quad, side], NT, preferred_element_type=F32)
            total = part if total is None else total + part
        for i in range(3):
            out[side, i] = total[128 * i : 128 * i + 128].astype(BF)


def cells(nodes, table, weights, shear, bulk, grads):
    vmem = pl.BlockSpec(memory_space=pltpu.VMEM)
    return pl.pallas_call(
        cells_kernel,
        name="cells",
        out_shape=jax.ShapeDtypeStruct((3, 3, 128, 256), BF),
        in_specs=[vmem] * 5 + [pl.BlockSpec(memory_space=pl.ANY)],
        out_specs=vmem,
        scratch_shapes=[
            pltpu.VMEM((32, 3, 192, 128), BF),
            pltpu.VMEM((3, 128, 128), F32),
            pltpu.VMEM((8, 8, QUAD), F32),
            pltpu.VMEM((8, 3, 256, QUAD), BF),
            pltpu.VMEM((8, 384, QUAD), BF),
            pltpu.SemaphoreType.DMA,
        ],
        compiler_params=pltpu.CompilerParams(vmem_limit_bytes=56 << 20),
    )(nodes, table, weights, shear, bulk, grads)


def finish_kernel(
    forces, now, prev, inv_mass, owner, block_nodes, phi_hbm, corr_hbm, target, fixed, out,
    got, summed, state, asking, asked, answer, answered, giving, given, adding, part, halves,
    phi, corr, phi_bf, corr_bf, goal, held, numbers, values, deltas, permuted, gathered,
    load_sem, force_send, force_recv, all_send, all_recv, ask_send, ask_recv, ans_send, ans_recv,
    give_send, give_recv, part_send, part_recv, half_send, half_recv,
):
    slab, group = lax.axis_index("slab"), lax.axis_index("group")
    slabs, groups = 16, 8

    def slab_at(by):
        return lax.rem(slab + by + slabs, slabs)

    def group_at(by):
        return lax.rem(group + by + groups, groups)

    barrier = pltpu.get_barrier_semaphore()

    def near_of(k):
        step = k + 1
        return step // groups, lax.rem(step, groups)

    def near_device(k):
        side, step = near_of(k)
        shift = jnp.where(side == 0, 0, jnp.where(side == 1, 1, -1))
        return slab_at(shift), group_at(step)

    def greet(k, carry):
        pl.semaphore_signal(barrier, inc=1, device_id=near_device(k), device_id_type=MESH)
        return carry

    def greet_far(k, carry):
        pl.semaphore_signal(barrier, inc=1, device_id=(slab_at(k), group), device_id_type=MESH)
        return carry

    lax.fori_loop(0, 23, greet, 0)
    lax.fori_loop(2, 15, greet_far, 0)
    load_phi = pltpu.make_async_copy(phi_hbm, phi, load_sem.at[0])
    load_corr = pltpu.make_async_copy(corr_hbm, corr, load_sem.at[1])
    load_own = pltpu.make_async_copy(
        forces.at[1, :, pl.ds(pl.multiple_of(group * 16, 16), 16), :], got.at[23], load_sem.at[2]
    )
    load_phi.start()
    load_corr.start()
    load_own.start()
    pl.semaphore_wait(barrier, 36)

    def force_copy(k):
        side, step = near_of(k)
        source = jnp.where(side == 0, 1, jnp.where(side == 1, 2, 0))
        start = pl.multiple_of(group_at(step) * 16, 16)
        return pltpu.make_async_remote_copy(
            src_ref=forces.at[source, :, pl.ds(start, 16), :],
            dst_ref=got.at[k],
            send_sem=force_send.at[k],
            recv_sem=force_recv.at[k],
            device_id=near_device(k),
            device_id_type=MESH,
        )

    def start_force(k, carry):
        force_copy(k).start()
        return carry

    lax.fori_loop(0, 23, start_force, 0)

    own_row = owner[...]
    diag = lax.broadcasted_iota(jnp.int32, (32, 32), 0) == lax.broadcasted_iota(jnp.int32, (32, 32), 1)
    own_col = jnp.sum(jnp.where(diag, own_row, 0), axis=1, keepdims=True)
    block_wide = lax.broadcasted_iota(jnp.int32, (32, 128), 0)
    of_lane = lax.broadcasted_iota(jnp.int32, (32, 128), 1) // 4
    own_wide = jnp.sum(jnp.where(block_wide == of_lane, own_col, 0), axis=0, keepdims=True)
    earlier = (own_col == own_wide) & (block_wide < of_lane)
    rank = jnp.sum(jnp.where(earlier, 1, 0), axis=0, keepdims=True)
    relative = own_wide - slab
    relative = jnp.where(relative < 0, relative + slabs, relative)
    key = relative * 16 + rank * 4 + lax.broadcasted_iota(jnp.int32, (1, 128), 1) % 4
    to_slots = onehot(key, 256)
    square = lax.broadcasted_iota(jnp.int32, (128, 128), 0) == lax.broadcasted_iota(jnp.int32, (128, 128), 1)
    key_col = jnp.sum(jnp.where(square, key, 0), axis=1, keepdims=True)
    to_blocks = jnp.where(lax.broadcasted_iota(jnp.int32, (128, 256), 1) == key_col, 1.0, 0.0).astype(BF)

    node = block_nodes[...]
    numbers[...] = jnp.zeros_like(numbers)
    for side in range(2):
        span = slice(128 * side, 128 * side + 128)
        numbers[side, pl.ds(0, 32, stride=4), :] = ((node[:, span] >> 8) + 1).astype(F32)
        numbers[side, pl.ds(1, 32, stride=4), :] = ((node[:, span] & 255) + 1).astype(F32)
    named = jnp.concatenate([numbers[0], numbers[1]], axis=1).astype(BF)
    asks = jnp.dot(to_slots, named, preferred_element_type=F32) - 1.0
    for q in range(16):
        asking[q] = asks[16 * q : 16 * q + 16].astype(BF)

    def exchange(source, landing, send, recv):
        def copy(q):
            return pltpu.make_async_remote_copy(
                src_ref=source.at[q],
                dst_ref=landing.at[slabs - q],
                send_sem=send.at[q],
                recv_sem=recv.at[slabs - q],
                device_id=(slab_at(q), group),
                device_id_type=MESH,
            )

        def arrival(q):
            return pltpu.make_async_remote_copy(
                src_ref=source.at[q],
                dst_ref=landing.at[q],
                send_sem=send.at[q],
                recv_sem=recv.at[q],
                device_id=(slab_at(q), group),
                device_id_type=MESH,
            )

        return copy, arrival

    ask_copy, ask_arrival = exchange(asking, asked, ask_send, ask_recv)
    ans_copy, ans_arrival = exchange(answer, answered, ans_send, ans_recv)
    give_copy, give_arrival = exchange(giving, given, give_send, give_recv)

    def start_ask(q, carry):
        ask_copy(q).start()
        return carry

    lax.fori_loop(1, 16, start_ask, 0)
    asked[0] = asking[0]
    for i in range(3):
        goal[pl.ds(i, 32, stride=4), :] = target[i]
    goal[pl.ds(3, 32, stride=4), :] = jnp.zeros((32, 128), F32)
    for i in range(4):
        held[pl.ds(i, 32, stride=4), :] = fixed[...].astype(F32)
    load_phi.wait()
    load_corr.wait()

    def narrow(pair, carry):
        phi_bf[pair] = phi[pair].astype(BF)
        corr_bf[pair] = corr[pair].astype(BF)
        return carry

    lax.fori_loop(0, 16, narrow, 0)
    load_own.wait()

    share = got[23].astype(F32)
    for k in range(23):
        force_copy(k).wait_recv()
        side = (k + 1) // groups
        piece = got[k].astype(F32)
        if side == 1:
            piece = jnp.where(slab == 0, 0.0, piece)
        if side == 2:
            piece = jnp.where(slab == slabs - 1, 0.0, piece)
        share = share + piece

    mine = pl.ds(pl.multiple_of(group * 16, 16), 16)

    def shared(buffer, send, recv):
        def copy(step):
            return pltpu.make_async_remote_copy(
                src_ref=buffer.at[:, mine, :],
                dst_ref=buffer.at[:, mine, :],
                send_sem=send.at[step],
                recv_sem=recv.at[groups - step],
                device_id=(slab, group_at(step)),
                device_id_type=MESH,
            )

        def arrival(step):
            theirs = pl.ds(pl.multiple_of(group_at(step) * 16, 16), 16)
            return pltpu.make_async_remote_copy(
                src_ref=buffer.at[:, theirs, :],
                dst_ref=buffer.at[:, theirs, :],
                send_sem=send.at[step],
                recv_sem=recv.at[step],
                device_id=(slab, group_at(step)),
                device_id_type=MESH,
            )

        return copy, arrival

    sum_copy, sum_arrival = shared(summed, all_send, all_recv)
    half_copy, half_arrival = shared(halves, half_send, half_recv)
    summed[:, mine, :] = share.astype(BF)
    for step in range(1, groups):
        sum_copy(step).start()
    for i in range(3):
        state[i] = 2.0 * now[i] - prev[i]
    for step in range(1, groups):
        sum_arrival(step).wait_recv()
    for i in range(3):
        state[i] = state[i] - inv_mass[...] * summed[i].astype(F32)
        gathered[128 * i : 128 * i + 128, :] = state[i].astype(BF)

    rows_of = lax.broadcasted_iota(jnp.int32, (128, 1024), 0)
    sixteen = lax.broadcasted_iota(jnp.int32, (16, 256), 0)

    def spots(q):
        spot = asked[q].astype(F32)
        row = jnp.concatenate([spot[4 * c : 4 * c + 1] for c in range(CAP)], axis=1).astype(jnp.int32)
        column = jnp.concatenate([spot[4 * c + 1 : 4 * c + 2] for c in range(CAP)], axis=1).astype(jnp.int32)
        return row, column

    def look(q):
        row, column = spots(q)
        hit = jnp.dot(gathered[...], onehot(column, 256), preferred_element_type=F32)
        mask = rows_of == row
        found = jnp.zeros((16, 256), F32)
        for i in range(3):
            line = jnp.sum(jnp.where(mask, hit[128 * i : 128 * i + 128], 0.0), axis=0, keepdims=True)
            for c in range(CAP):
                found = jnp.where(sixteen == 4 * c + i, line[:, 256 * c : 256 * c + 256], found)
        answer[q] = found.astype(BF)

    def look_far(q, carry):
        ask_arrival(q).wait_recv()
        look(q)
        ans_copy(q).start()
        return carry

    lax.fori_loop(1, 16, look_far, 0)
    look(0)
    permuted[0:16] = answer[0]

    def take(q, carry):
        ans_arrival(q).wait_recv()
        permuted[pl.ds(pl.multiple_of(q * 16, 16), 16), :] = answered[q]
        return carry

    lax.fori_loop(1, 16, take, 0)
    values[...] = jnp.dot(to_blocks, permuted[...], preferred_element_type=F32)

    upper = lax.broadcasted_iota(jnp.int32, (8, 128), 0) < 4

    def correct(pair, carry):
        at = pl.ds(pl.multiple_of(8 * pair, 8), 8)
        both = lax.dot_general(values[at, :].astype(BF), phi_bf[pair], NT, preferred_element_type=F32)
        interp = jnp.where(upper, both[:, :128], both[:, 128:])
        resid = held[at, :] * (goal[at, :] - interp)
        both = lax.dot_general(resid.astype(BF), corr_bf[pair], NT, preferred_element_type=F32)
        wide = jnp.concatenate([jnp.where(upper, both[:, :128], 0.0), jnp.where(upper, 0.0, both[:, 128:])], axis=1)
        deltas[at, :] = jnp.dot(wide.astype(BF), phi_bf[pair], preferred_element_type=F32)
        return carry

    lax.fori_loop(0, 16, correct, 0)
    gives = jnp.dot(to_slots, deltas[...].astype(BF), preferred_element_type=F32).astype(BF)
    for q in range(16):
        giving[q] = gives[16 * q : 16 * q + 16]

    def start_give(q, carry):
        give_copy(q).start()
        return carry

    lax.fori_loop(1, 16, start_give, 0)
    given[0] = giving[0]

    def place(q):
        row, column = spots(q)
        mask = rows_of == row
        amount = given[q].astype(F32)
        lines = []
        for i in range(3):
            line = jnp.concatenate([amount[4 * c + i : 4 * c + i + 1] for c in range(CAP)], axis=1)
            lines.append(jnp.where(mask, line, 0.0).astype(BF))
        return lax.dot_general(
            jnp.concatenate(lines, axis=0), onehot(column, 256), NT, preferred_element_type=F32
        )

    adding[...] = place(0)

    def place_far(q, carry):
        give_arrival(q).wait_recv()
        adding[...] += place(q)
        return carry

    lax.fori_loop(1, 16, place_far, 0)
    for i in range(3):
        part[0, i] = adding[128 * i : 128 * i + 128, :].astype(BF)

    def part_copy(step):
        theirs = pl.ds(pl.multiple_of(group_at(step) * 16, 16), 16)
        return pltpu.make_async_remote_copy(
            src_ref=part.at[0, :, theirs, :],
            dst_ref=got.at[24 + groups - step],
            send_sem=part_send.at[step],
            recv_sem=part_recv.at[groups - step],
            device_id=(slab, group_at(step)),
            device_id_type=MESH,
        )

    def part_arrival(step):
        theirs = pl.ds(pl.multiple_of(group_at(step) * 16, 16), 16)
        return pltpu.make_async_remote_copy(
            src_ref=part.at[0, :, theirs, :],
            dst_ref=got.at[24 + step],
            send_sem=part_send.at[step],
            recv_sem=part_recv.at[step],
            device_id=(slab, group_at(step)),
            device_id_type=MESH,
        )

    for step in range(1, groups):
        part_copy(step).start()
    share = jnp.stack([adding[pl.ds(pl.multiple_of(128 * i + group * 16, 16), 16), :] for i in range(3)])
    for step in range(1, groups):
        part_arrival(step).wait_recv()
        share = share + got[24 + step].astype(F32)
    halves[:, mine, :] = share.astype(BF)
    for step in range(1, groups):
        half_copy(step).start()
    for step in range(1, groups):
        half_arrival(step).wait_recv()
    for i in range(3):
        out[i] = state[i] + halves[i].astype(F32)

    def end_force(k, carry):
        force_copy(k).wait_send()
        return carry

    def end_far(q, carry):
        ask_copy(q).wait_send()
        ans_copy(q).wait_send()
        give_copy(q).wait_send()
        return carry

    def end_near(step, carry):
        sum_copy(step).wait_send()
        part_copy(step).wait_send()
        half_copy(step).wait_send()
        return carry

    lax.fori_loop(0, 23, end_force, 0)
    lax.fori_loop(1, 16, end_far, 0)
    lax.fori_loop(1, groups, end_near, 0)


def finish(forces, now, prev, inv_mass, owner, block_nodes, phi, corr, target, fixed):
    vmem = pl.BlockSpec(memory_space=pltpu.VMEM)
    anywhere = pl.BlockSpec(memory_space=pl.ANY)
    dma = pltpu.SemaphoreType.DMA
    message = pltpu.VMEM((16, 16, 256), BF)
    nodal = pltpu.VMEM((3, 128, 256), BF)
    return pl.pallas_call(
        finish_kernel,
        name="finish",
        out_shape=jax.ShapeDtypeStruct((3, 128, 256), F32),
        in_specs=[anywhere] + [vmem] * 5 + [anywhere] * 2 + [vmem] * 2,
        out_specs=vmem,
        scratch_shapes=[
            pltpu.VMEM((32, 3, 16, 256), BF),
            nodal,
            pltpu.VMEM((3, 128, 256), F32),
            message, message, message, message, message, message,
            pltpu.VMEM((384, 256), F32),
            pltpu.VMEM((1, 3, 128, 256), BF),
            nodal,
            pltpu.VMEM((16, 256, 256), F32),
            pltpu.VMEM((16, 256, 128), F32),
            pltpu.VMEM((16, 256, 256), BF),
            pltpu.VMEM((16, 256, 128), BF),
            pltpu.VMEM((128, 128), F32),
            pltpu.VMEM((128, 128), F32),
            pltpu.VMEM((2, 128, 128), F32),
            pltpu.VMEM((128, 256), F32),
            pltpu.VMEM((128, 256), F32),
            pltpu.VMEM((256, 256), BF),
            pltpu.VMEM((384, 256), BF),
            dma((3,)), dma((23,)), dma((23,)), dma((8,)), dma((8,)), dma((16,)), dma((16,)), dma((16,)), dma((16,)),
            dma((16,)), dma((16,)), dma((8,)), dma((8,)), dma((8,)), dma((8,)),
        ],
        compiler_params=pltpu.CompilerParams(
            vmem_limit_bytes=48 << 20, collective_id=0, has_side_effects=True
        ),
    )(forces, now, prev, inv_mass, owner, block_nodes, phi, corr, target, fixed)


def body(
    disp_now, disp_prev, inv_mass, cell_nodes, shape_grads, cell_weights, cell_shear, cell_bulk,
    block_owner, block_nodes, block_phi, block_corr, block_target, block_fixed,
):
    own = disp_now.astype(BF).reshape(384, 256)
    count = lax.axis_size("slab")
    forward = [(i, i + 1) for i in range(count - 1)]
    backward = [(b, a) for a, b in forward]
    low = lax.ppermute(own, "slab", forward)
    high = lax.ppermute(own, "slab", backward)
    table = jnp.stack([low, own, high])
    forces = cells(
        cell_nodes.reshape(8, 1, QUAD), table, cell_weights, cell_shear[:, None], cell_bulk[:, None], shape_grads
    )
    result = finish(
        forces,
        disp_now.reshape(3, 128, 256),
        disp_prev.reshape(3, 128, 256),
        inv_mass.reshape(128, 256),
        block_owner.reshape(1, 32),
        block_nodes,
        block_phi.reshape(16, 256, 256),
        block_corr.reshape(16, 256, 128),
        jnp.moveaxis(block_target, 1, 0),
        block_fixed,
    )
    return result.reshape(3, 32768)


def solution(mesh):
    both = ("slab", "group")
    placed = (
        P(None, "slab"), P(None, "slab"), P("slab"), P(both, None), P(both, None, None, None), P(both, None),
        P(both), P(both), P(both, None), P(both, None), P(both, None, None), P(both, None, None),
        P(both, None, None), P(both, None),
    )
    return jax.shard_map(body, mesh=mesh, in_specs=placed, out_specs=P(None, "slab"), check_vma=False)
```

time: 564 us -> 95.6 us (0.17)
  other arithmetic: 171 us -> 2.01 us
  local copies, waits for them, and re-layouts: 173 us -> 10.1 us
  waiting for transfers between devices: 142 us -> 0.01 us
  Pallas kernels: 0 us -> 76.9 us
  blocking collectives: 24.4 us -> 0 us
  matrix products: 18.6 us -> 0 us
  starting transfers between devices: 20.1 us -> 5.96 us
  between operations: 13.7 us -> 0.16 us
    scatter-add x2 -> x0, other arithmetic: 160 us -> none  [the longest x1 107 us: body(): jnp.zeros((3, width), jnp.float32).at[:, asked]]
    psum x2 -> x0, waiting for transfers between devices: 123 us -> none  [the longest x1 70.7 us: body(): return disp_next + lax.psum(added, 'group')]
    gather x5 -> x0, local copies, waits for them, and re-layouts: 101 us -> none  [the longest x2 65.5 us: body(): looked = jnp.moveaxis(jnp.take(disp_next, asked, axis=1), 0, 2)]
    pallas_call x0 -> x2, Pallas kernels: none -> 76.9 us  [the longest x1 60.2 us: finish(): pl.pallas_call(finish_kernel, name='finish', out_shape=jax.ShapeDtypeStru...]
    scatter-add x2 -> x0, local copies, waits for them, and re-layouts: 36.5 us -> none  [the longest x1 26.7 us: body(): jnp.zeros((3, 3 * width), jnp.float32).at[:, cell_nodes]]
    all_to_all x2 -> x0, blocking collectives: 24.4 us -> none  [the longest x1 14.3 us: body(): lax.all_to_all(request, 'slab', split_axis=0, concat_axis=0, tiled=True)]
    dot_general x5 -> x0, matrix products: 18.6 us -> none  [the longest x1 5.84 us: body(): interp = jnp.einsum('bma,bia->bim', block_phi, values, precision=highest)]
    concatenate x1 -> x0, local copies, waits for them, and re-layouts: 15.8 us -> none  [extended(): block = jnp.concatenate([low, block, high], axis=dim)]
  transfers between devices with their start and end apart: 7 -> 2, of which waited for: 7 -> 0; matrix products, arithmetic and copies ran while one was open for 1% -> 8% of each run, Pallas kernels for 0% -> 0%
where the time goes in v1:
time: 95.6 us; the launch traced here: 95.2 us
  Pallas kernels  76.9 us (80%)
  local copies, waits for them, and re-layouts  10.1 us (11%)
  starting transfers between devices  5.96 us (6%)
  other arithmetic  2.01 us (2%)
    pallas_call x1, Pallas kernels, finish(): pl.pallas_call(finish_kernel, name='finish', out_shape=jax.ShapeDtypeStru...  60.2 us
    pallas_call x1, Pallas kernels, cells(): pl.pallas_call(cells_kernel, name='cells', out_shape=jax.ShapeDtypeStruct...  16.6 us
    ppermute x1, starting transfers between devices, body(): low = lax.ppermute(own, 'slab', forward)  4.67 us
    unnamed x15, local copies, waits for them, and re-layouts  4.53 us
  transfers between devices with their start and end apart: 2, of which 0 were waited for; matrix products, arithmetic and copies ran while one was open for 8% of the time, Pallas kernels for 0%

profile of v1, /device:TPU:1, one launch (start us, length us, event | category | flops | bytes accessed | tf_op | source)
XLA Modules:
  0.0 95.2 jit_solution(1226636416731837461)
XLA Ops:
  0.0 1.1 %convert_element_type.3 = bf16[3,32768]{1,0:T(4,128)(2,1)S(1)} convert(f32[3,32768]{1,0:T(4,128)} %param.14) | non-fusion elementwise | flops 98304 | bytes 589824 | tf_op jit(solution)/shard_map/convert_element_type | solution.py:508
  1.1 0.3 reshape.28
  1.4 1.3 %collective-permute-start.1 = (bf16[384,256]{1,0:T(8,128)(2,1)S(1)}, bf16[384,256]{1,0:T(8,128)(2,1)S(1)}, u32[]{:S(2)}, u32[]{:S(2)}) collective-permute-start(bf16[384,256]{1,0:T(8,128)(2,1)S(1)} %reshape.28), channel_id=1, source_target_pairs={{8,0},{16,8},{24,16},{32,24},{40,32},{48,40},{56,48},{64,56},{72,6... | collective-permute-start | bytes 589832 | tf_op jit(solution)/shard_map/ppermute | solution.py:513
  2.7 4.7 %collective-permute-start = (bf16[384,256]{1,0:T(8,128)(2,1)S(1)}, bf16[384,256]{1,0:T(8,128)(2,1)S(1)}, u32[]{:S(2)}, u32[]{:S(2)}) collective-permute-start(bf16[384,256]{1,0:T(8,128)(2,1)S(1)} %reshape.28), channel_id=1, source_target_pairs={{0,8},{8,16},{16,24},{24,32},{32,40},{40,48},{48,56},{56,64},{64,7... | collective-permute-start | bytes 589832 | tf_op jit(solution)/shard_map/ppermute | solution.py:512
  7.4 0.3 stack_reshape.3
  7.7 1.3 %copy.15.shear = f32[32,1]{1,0:T(8,128)} copy(f32[32,1]{0,1:T(1,128)} %bitcast.29) | data formatting | bytes 256 | tf_op jit(solution)/shard_map/broadcast_in_dim | solution.py:516
  9.0 1.3 %copy.16.bulk = f32[32,1]{1,0:T(8,128)} copy(f32[32,1]{0,1:T(1,128)} %bitcast.30) | data formatting | bytes 256 | tf_op jit(solution)/shard_map/broadcast_in_dim | solution.py:516
  10.3 1.5 %reshape.27.nodes = s32[8,1,768]{2,1,0:T(1,128)} reshape(s32[32,192]{1,0:T(8,128)} %param.17) | data formatting | bytes 49152 | tf_op jit(solution)/shard_map/reshape | solution.py:516
  11.8 0.9 reshape.31.inv_mass
  12.7 1.1 %copy.22 = f32[1,3,128,256]{3,2,1,0:T(8,128)S(1)} copy(f32[1,3,128,256]{3,1,2,0:T(4,128)} %bitcast.26) | data formatting | bytes 786432
  13.9 0.0 copy-start.1
  13.9 0.0 copy-start.2
  13.9 0.0 copy-start.3
  13.9 0.0 copy-start.4
  13.9 0.0 copy-start.5
  13.9 1.3 %copy.23 = f32[1,3,128,256]{3,2,1,0:T(8,128)S(1)} copy(f32[1,3,128,256]{3,1,2,0:T(4,128)} %bitcast.25) | data formatting | bytes 786432
  15.2 0.0 collective-permute-done.1
  15.2 0.0 collective-permute-done
  15.2 0.9 pad_maximum_fusion.table
  16.1 16.6 %cells.1.forces = bf16[3,3,128,256]{3,2,1,0:T(8,128)(2,1)} custom-call(s32[8,1,768]{2,1,0:T(1,128)} %reshape.27.nodes, bf16[3,384,256]{2,1,0:T(8,128)(2,1)} %pad_maximum_fusion.table, f32[32,128]{1,0:T(8,128)} %weights.1, f32[32,1]{1,0:T(8,128)} %copy.15.shear, f32[32,1]{1,0:T(8,128)} %copy.16.bulk, bf16[32,3,192,128]{3,2,1,0:T(8,128)(2,1)} %grads_hbm.1), custom_call_target="tpu_custom_call" | custom-call | tf_op jit(solution)/shard_map/cells/pallas_call | solution.py:112
  32.7 0.0 copy-done.1
  32.7 0.0 copy-done.2
  32.7 0.0 copy-done.3
  32.7 0.0 copy-done.4
  32.8 0.0 copy-done.5
  32.8 0.0 copy-start
  32.8 1.1 %copy-done = bf16[3,3,128,256]{3,2,1,0:T(8,128)(2,1)S(1)} copy-done((bf16[3,3,128,256]{3,2,1,0:T(8,128)(2,1)S(1)}, bf16[3,3,128,256]{3,2,1,0:T(8,128)(2,1)}, u32[]{:S(2)}) %copy-start) | copy-done | bytes 589848
  33.8 60.2 %finish.1 = f32[3,128,256]{2,1,0:T(8,128)S(1)} custom-call(bf16[3,3,128,256]{3,2,1,0:T(8,128)(2,1)S(1)} %copy-done, f32[3,128,256]{2,1,0:T(8,128)S(1)} %bitcast.20, f32[3,128,256]{2,1,0:T(8,128)S(1)} %bitcast.19, f32[128,256]{1,0:T(8,128)S(1)} %reshape.31.inv_mass, s32[1,32]{1,0:T(1,128)S(1)} %bitcast.23, s32[32,256]{1,0:T(8,128)S(1)} %copy-done.3, ...), custom_call_target="tpu_custom_call" | custom-call | tf_op jit(solution)/shard_map/finish/pallas_call | solution.py:470
  94.1 1.1 %copy.19 = f32[1,3,128,256]{3,1,2,0:T(4,128)} copy(f32[1,3,128,256]{3,2,1,0:T(8,128)S(1)} %bitcast.21) | data formatting | bytes 786432
Async XLA Ops:
  1.4 13.8 %collective-permute-start.1 = (bf16[384,256]{1,0:T(8,128)(2,1)S(1)}, bf16[384,256]{1,0:T(8,128)(2,1)S(1)}, u32[]{:S(2)}, u32[]{:S(2)}) collective-permute-start(bf16[384,256]{1,0:T(8,128)(2,1)S(1)} %reshape.28), channel_id=1, source_target_pairs={{8,0},{16,8},{24,16},{32,24},{40,32},{48,40},{56,48},{64,56},{72,6... | collective-permute-start | bytes 589832 | tf_op jit(solution)/shard_map/ppermute | solution.py:513
  2.7 12.5 %collective-permute-start = (bf16[384,256]{1,0:T(8,128)(2,1)S(1)}, bf16[384,256]{1,0:T(8,128)(2,1)S(1)}, u32[]{:S(2)}, u32[]{:S(2)}) collective-permute-start(bf16[384,256]{1,0:T(8,128)(2,1)S(1)} %reshape.28), channel_id=1, source_target_pairs={{0,8},{8,16},{16,24},{24,32},{32,40},{40,48},{48,56},{56,64},{64,7... | collective-permute-start | bytes 589832 | tf_op jit(solution)/shard_map/ppermute | solution.py:512
  13.9 18.9 %copy-start.1 = (f32[32,128,128]{2,1,0:T(8,128)S(1)}, f32[32,128,128]{2,1,0:T(8,128)}, u32[]{:S(2)}) copy-start(f32[32,128,128]{2,1,0:T(8,128)} %param.25) | copy-start | bytes 6291460
  13.9 18.9 %copy-start.2 = (f32[32,3,128]{2,0,1:T(8,128)S(1)}, f32[32,3,128]{2,0,1:T(8,128)}, u32[]{:S(2)}) copy-start(f32[32,3,128]{2,0,1:T(8,128)} %param.26) | copy-start | bytes 147460
  13.9 18.9 %copy-start.3 = (s32[32,256]{1,0:T(8,128)S(1)}, s32[32,256]{1,0:T(8,128)}, u32[]{:S(2)}) copy-start(s32[32,256]{1,0:T(8,128)} %block_nodes.1) | copy-start | bytes 98308
  13.9 18.9 %copy-start.4 = (s32[32,128]{1,0:T(8,128)S(1)}, s32[32,128]{1,0:T(8,128)}, u32[]{:S(2)}) copy-start(s32[32,128]{1,0:T(8,128)} %fixed.1) | copy-start | bytes 49156
  13.9 18.8 %copy-start.5 = (s32[32,1]{0,1:T(1,128)S(1)}, s32[32,1]{0,1:T(1,128)}, u32[]{:S(2)}) copy-start(s32[32,1]{0,1:T(1,128)} %param.22) | copy-start | bytes 388
  32.8 1.1 %copy-start = (bf16[3,3,128,256]{3,2,1,0:T(8,128)(2,1)S(1)}, bf16[3,3,128,256]{3,2,1,0:T(8,128)(2,1)}, u32[]{:S(2)}) copy-start(bf16[3,3,128,256]{3,2,1,0:T(8,128)(2,1)} %cells.1.forces) | copy-start | bytes 1769476

commit v2 on v1

v2 whole, which is shorter than its diff:
```python
import jax
import jax.numpy as jnp
from jax import lax
from jax.experimental import pallas as pl
from jax.experimental.pallas import tpu as pltpu
from jax.sharding import PartitionSpec as P

BF = jnp.bfloat16
F32 = jnp.float32
NT = (((1,), (1,)), ((), ()))
MESH = pl.DeviceIdType.MESH
CAP = 4
QUAD = 768


def onehot(index, size):
    rows = lax.broadcasted_iota(jnp.int32, (size, index.shape[1]), 0)
    return jnp.where(rows == index, 1.0, 0.0).astype(BF)


def step_kernel(
    now_hbm, prev_hbm, mass_hbm, cell_nodes, grads_hbm, weights, shear, bulk, owner, block_nodes, phi_hbm, corr_hbm,
    target, fixed, out,
    lines, prev, mass, state, tables, nodes, grads, field, near, columns, spread, forces,
    got, summed, asking, asked, answer, answered, giving, given, adding, part, halves,
    phi, corr, phi_bf, corr_bf, goal, held, numbers, values, resids, permuted, gathered, hots,
    load_sem, halo_send, halo_recv, force_send, force_recv, all_send, all_recv, ask_send, ask_recv, ans_send, ans_recv,
    give_send, give_recv, part_send, part_recv, half_send, half_recv,
):
    slab, group = lax.axis_index("slab"), lax.axis_index("group")
    slabs, groups = 16, 8

    def slab_at(by):
        return lax.rem(slab + by + slabs, slabs)

    def group_at(by):
        return lax.rem(group + by + groups, groups)

    load_now = pltpu.make_async_copy(now_hbm, lines, load_sem.at[0])
    load_grads = pltpu.make_async_copy(grads_hbm, grads, load_sem.at[1])
    load_prev = pltpu.make_async_copy(prev_hbm, prev, load_sem.at[2])
    load_mass = pltpu.make_async_copy(mass_hbm, mass, load_sem.at[3])
    load_phi = pltpu.make_async_copy(phi_hbm, phi, load_sem.at[4])
    load_corr = pltpu.make_async_copy(corr_hbm, corr, load_sem.at[5])
    load_now.start()
    load_grads.start()
    load_prev.start()
    load_mass.start()
    load_phi.start()
    load_corr.start()

    barrier = pltpu.get_barrier_semaphore()

    def near_device(k):
        shift = jnp.where(k < 8, -1, jnp.where(k < 16, 1, 0))
        return slab_at(shift), group_at(lax.rem(k + 1, groups))

    def greet(k, carry):
        pl.semaphore_signal(barrier, inc=1, device_id=near_device(k), device_id_type=MESH)
        return carry

    def greet_far(k, carry):
        pl.semaphore_signal(barrier, inc=1, device_id=(slab_at(k), group), device_id_type=MESH)
        return carry

    lax.fori_loop(0, 23, greet, 0)
    lax.fori_loop(2, 15, greet_far, 0)

    def relaid(source, use):
        def move(block, carry):
            start = pl.multiple_of(block * 2048, 2048)
            wide = source[:, pl.ds(start, 2048)]
            at = pl.ds(pl.multiple_of(block * 8, 8), 8)
            for i in range(3):
                use(i, at, jnp.concatenate([wide[i : i + 1, 256 * r : 256 * r + 256] for r in range(8)], axis=0))
            return carry

        lax.fori_loop(0, 16, move, 0)

    def set_state(i, at, value):
        state[i, at, :] = value

    load_now.wait()
    relaid(lines, set_state)
    for i in range(3):
        tables[1, 128 * i : 128 * i + 128, :] = state[i].astype(BF)
    pl.semaphore_wait(barrier, 36)

    def halo(side, by):
        return pltpu.make_async_remote_copy(
            src_ref=tables.at[1],
            dst_ref=tables.at[side],
            send_sem=halo_send.at[side],
            recv_sem=halo_recv.at[side],
            device_id=(slab_at(by), group),
            device_id_type=MESH,
        )

    to_above, to_below = halo(0, 1), halo(2, -1)
    to_above.start()
    to_below.start()

    own_row = owner[...]
    diag = lax.broadcasted_iota(jnp.int32, (32, 32), 0) == lax.broadcasted_iota(jnp.int32, (32, 32), 1)
    own_col = jnp.sum(jnp.where(diag, own_row, 0), axis=1, keepdims=True)
    block_wide = lax.broadcasted_iota(jnp.int32, (32, 128), 0)
    of_lane = lax.broadcasted_iota(jnp.int32, (32, 128), 1) // 4
    own_wide = jnp.sum(jnp.where(block_wide == of_lane, own_col, 0), axis=0, keepdims=True)
    earlier = (own_col == own_wide) & (block_wide < of_lane)
    rank = jnp.sum(jnp.where(earlier, 1, 0), axis=0, keepdims=True)
    relative = own_wide - slab
    relative = jnp.where(relative < 0, relative + slabs, relative)
    key = relative * 16 + rank * 4 + lax.broadcasted_iota(jnp.int32, (1, 128), 1) % 4
    to_slots = onehot(key, 256)
    square = lax.broadcasted_iota(jnp.int32, (128, 128), 0) == lax.broadcasted_iota(jnp.int32, (128, 128), 1)
    key_col = jnp.sum(jnp.where(square, key, 0), axis=1, keepdims=True)

    node = block_nodes[...]
    numbers[...] = jnp.zeros_like(numbers)
    for side in range(2):
        span = slice(128 * side, 128 * side + 128)
        numbers[side, pl.ds(0, 32, stride=4), :] = ((node[:, span] >> 8) + 1).astype(F32)
        numbers[side, pl.ds(1, 32, stride=4), :] = ((node[:, span] & 255) + 1).astype(F32)
    named = jnp.concatenate([numbers[0], numbers[1]], axis=1).astype(BF)
    asks = jnp.dot(to_slots, named, preferred_element_type=F32) - 1.0
    for q in range(16):
        asking[q] = asks[16 * q : 16 * q + 16].astype(BF)

    def exchange(source, landing, send, recv):
        def copy(q):
            return pltpu.make_async_remote_copy(
                src_ref=source.at[q],
                dst_ref=landing.at[slabs - q],
                send_sem=send.at[q],
                recv_sem=recv.at[slabs - q],
                device_id=(slab_at(q), group),
                device_id_type=MESH,
            )

        def arrival(q):
            return pltpu.make_async_remote_copy(
                src_ref=source.at[q],
                dst_ref=landing.at[q],
                send_sem=send.at[q],
                recv_sem=recv.at[q],
                device_id=(slab_at(q), group),
                device_id_type=MESH,
            )

        return copy, arrival

    ask_copy, ask_arrival = exchange(asking, asked, ask_send, ask_recv)
    ans_copy, ans_arrival = exchange(answer, answered, ans_send, ans_recv)
    give_copy, give_arrival = exchange(giving, given, give_send, give_recv)

    def start_ask(q, carry):
        ask_copy(q).start()
        return carry

    lax.fori_loop(1, 16, start_ask, 0)
    asked[0] = asking[0]

    def flatten(quad, carry):
        rows = [cell_nodes[pl.ds(4 * quad + e, 1), :] for e in range(4)]
        nodes[quad] = jnp.concatenate(rows, axis=1)
        return carry

    lax.fori_loop(0, 8, flatten, 0)
    rows_quad = lax.broadcasted_iota(jnp.int32, (128, QUAD), 0)

    def pick(total, row):
        mask = rows_quad == row
        return [
            jnp.sum(jnp.where(mask, total[128 * i : 128 * i + 128], 0.0), axis=0, keepdims=True) for i in range(3)
        ]

    def gather_own(quad, carry):
        number = nodes[quad]
        side_of, row, column = number >> 15, (number >> 8) & 127, number & 255
        for side in range(3):
            columns[quad, side] = onehot(jnp.where(side_of == side, column, -1), 256)
        total = jnp.dot(tables[1], columns[quad, 1], preferred_element_type=F32)
        for i, line in enumerate(pick(total, row)):
            near[quad, i : i + 1, :] = line
        return carry

    lax.fori_loop(0, 8, gather_own, 0)
    to_above.wait_recv()
    to_below.wait_recv()
    tables[0] = jnp.where(slab == 0, 0.0, tables[0].astype(F32)).astype(BF)
    tables[2] = jnp.where(slab == slabs - 1, 0.0, tables[2].astype(F32)).astype(BF)

    def gather_sides(quad, carry):
        row = (nodes[quad] >> 8) & 127
        total = jnp.dot(tables[0], columns[quad, 0], preferred_element_type=F32)
        total += jnp.dot(tables[2], columns[quad, 2], preferred_element_type=F32)
        for i, line in enumerate(pick(total, row)):
            near[quad, i : i + 1, :] += line
        return carry

    lax.fori_loop(0, 8, gather_sides, 0)
    load_grads.wait()
    sub = lax.broadcasted_iota(jnp.int32, (8, 384), 0)
    lane = lax.broadcasted_iota(jnp.int32, (8, 384), 1)
    own = (sub >= 4) == (lane >= 192)

    def gradient(quad, carry):
        for pair in range(2):
            left = jnp.zeros((8, 384), F32)
            for i in range(3):
                left = jnp.where(sub % 4 == i, near[quad, i : i + 1, 384 * pair : 384 * pair + 384], left)
            left = jnp.where(own, left, 0.0).astype(BF)
            for j in range(3):
                first = 4 * quad + 2 * pair
                both = jnp.concatenate([grads[first, j], grads[first + 1, j]], axis=0)
                at = pl.ds(pl.multiple_of(16 * quad + 8 * pair, 8), 8)
                field[j, at, :] = jnp.dot(left, both, preferred_element_type=F32)
        return carry

    lax.fori_loop(0, 8, gradient, 0)
    full = [
        [field[j, pl.ds(i, 32, stride=4), :] + (1.0 if i == j else 0.0) for j in range(3)]
        for i in range(3)
    ]
    cofactor = [
        [
            full[(i + 1) % 3][(j + 1) % 3] * full[(i + 2) % 3][(j + 2) % 3]
            - full[(i + 1) % 3][(j + 2) % 3] * full[(i + 2) % 3][(j + 1) % 3]
            for j in range(3)
        ]
        for i in range(3)
    ]
    volume = full[0][0] * cofactor[0][0] + full[0][1] * cofactor[0][1] + full[0][2] * cofactor[0][2]
    clamped = jnp.maximum(volume, 0.3)
    mu = jnp.sum(jnp.where(diag, shear[...], 0.0), axis=1, keepdims=True)
    lam = jnp.sum(jnp.where(diag, bulk[...], 0.0), axis=1, keepdims=True)
    weight = weights[...]
    factor = (lam * jnp.log(clamped) - mu) / clamped
    for i in range(3):
        for j in range(3):
            field[j, pl.ds(i, 32, stride=4), :] = weight * (mu * full[i][j] + factor * cofactor[i][j])
    low_lane = lax.broadcasted_iota(jnp.int32, (1, 384), 1) < 192
    rows_pair = lax.broadcasted_iota(jnp.int32, (128, 384), 0)

    def cell_forces(quad, carry):
        for pair in range(2):
            total = None
            for j in range(3):
                first = 4 * quad + 2 * pair
                at = pl.ds(pl.multiple_of(16 * quad + 8 * pair, 8), 8)
                both = jnp.concatenate([grads[first, j], grads[first + 1, j]], axis=0)
                piece = lax.dot_general(field[j, at, :].astype(BF), both, NT, preferred_element_type=F32)
                total = piece if total is None else total + piece
            span = slice(384 * pair, 384 * pair + 384)
            mask = rows_pair == ((nodes[quad, :, span] >> 8) & 127)
            for i in range(3):
                value = jnp.where(low_lane, total[i : i + 1], total[4 + i : 5 + i])
                spread[quad, 128 * i : 128 * i + 128, span] = jnp.where(mask, value, 0.0).astype(BF)
        return carry

    lax.fori_loop(0, 8, cell_forces, 0)

    def force_copy(k):
        source = jnp.where(k < 8, 0, jnp.where(k < 16, 2, 1))
        start = pl.multiple_of(group_at(lax.rem(k + 1, groups)) * 16, 16)
        return pltpu.make_async_remote_copy(
            src_ref=forces.at[source, :, pl.ds(start, 16), :],
            dst_ref=got.at[k],
            send_sem=force_send.at[k],
            recv_sem=force_recv.at[k],
            device_id=near_device(k),
            device_id_type=MESH,
        )

    def start_force(k, carry):
        force_copy(k).start()
        return carry

    for side, first, last in ((0, 0, 8), (2, 8, 16), (1, 16, 23)):
        total = None
        for quad in range(8):
            piece = lax.dot_general(spread[quad], columns[quad, side], NT, preferred_element_type=F32)
            total = piece if total is None else total + piece
        for i in range(3):
            forces[side, i] = total[128 * i : 128 * i + 128].astype(BF)
        lax.fori_loop(first, last, start_force, 0)

    load_prev.wait()

    def set_base(i, at, value):
        state[i, at, :] = 2.0 * state[i, at, :] - value

    relaid(prev, set_base)

    def spots(q):
        spot = asked[q].astype(F32)
        row = jnp.concatenate([spot[4 * c : 4 * c + 1] for c in range(CAP)], axis=1).astype(jnp.int32)
        column = jnp.concatenate([spot[4 * c + 1 : 4 * c + 2] for c in range(CAP)], axis=1).astype(jnp.int32)
        return row, column

    def heat(q):
        hots[q] = onehot(spots(q)[1], 256)

    def heat_far(q, carry):
        ask_arrival(q).wait_recv()
        heat(q)
        return carry

    heat(0)
    lax.fori_loop(1, 16, heat_far, 0)
    for i in range(3):
        goal[pl.ds(i, 32, stride=4), :] = target[i]
    goal[pl.ds(3, 32, stride=4), :] = jnp.zeros((32, 128), F32)
    for i in range(4):
        held[pl.ds(i, 32, stride=4), :] = fixed[...].astype(F32)
    load_phi.wait()
    load_corr.wait()

    def narrow(pair, carry):
        phi_bf[pair] = phi[pair].astype(BF)
        corr_bf[pair] = corr[pair].astype(BF)
        return carry

    lax.fori_loop(0, 16, narrow, 0)
    load_mass.wait()

    mine = pl.ds(pl.multiple_of(group * 16, 16), 16)
    share = forces[1, :, mine, :].astype(F32)
    for k in range(23):
        force_copy(k).wait_recv()
        piece = got[k].astype(F32)
        if k < 8:
            piece = jnp.where(slab == slabs - 1, 0.0, piece)
        elif k < 16:
            piece = jnp.where(slab == 0, 0.0, piece)
        share = share + piece

    def shared(buffer, send, recv):
        def copy(step):
            return pltpu.make_async_remote_copy(
                src_ref=buffer.at[:, mine, :],
                dst_ref=buffer.at[:, mine, :],
                send_sem=send.at[step],
                recv_sem=recv.at[groups - step],
                device_id=(slab, group_at(step)),
                device_id_type=MESH,
            )

        def arrival(step):
            theirs = pl.ds(pl.multiple_of(group_at(step) * 16, 16), 16)
            return pltpu.make_async_remote_copy(
                src_ref=buffer.at[:, theirs, :],
                dst_ref=buffer.at[:, theirs, :],
                send_sem=send.at[step],
                recv_sem=recv.at[step],
                device_id=(slab, group_at(step)),
                device_id_type=MESH,
            )

        return copy, arrival

    sum_copy, sum_arrival = shared(summed, all_send, all_recv)
    half_copy, half_arrival = shared(halves, half_send, half_recv)
    summed[:, mine, :] = share.astype(BF)
    for step in range(1, groups):
        sum_copy(step).start()
    scale = jnp.concatenate([mass[pl.ds(0, 128, stride=2), :], mass[pl.ds(1, 128, stride=2), :]], axis=1)
    for step in range(1, groups):
        sum_arrival(step).wait_recv()
    for i in range(3):
        state[i] = state[i] - scale * summed[i].astype(F32)
        gathered[128 * i : 128 * i + 128, :] = state[i].astype(BF)

    rows_of = lax.broadcasted_iota(jnp.int32, (128, 1024), 0)
    sixteen = lax.broadcasted_iota(jnp.int32, (16, 256), 0)

    def look(q):
        row, _ = spots(q)
        hit = jnp.dot(gathered[...], hots[q], preferred_element_type=F32)
        mask = rows_of == row
        found = jnp.zeros((16, 256), F32)
        for i in range(3):
            line = jnp.sum(jnp.where(mask, hit[128 * i : 128 * i + 128], 0.0), axis=0, keepdims=True)
            for c in range(CAP):
                found = jnp.where(sixteen == 4 * c + i, line[:, 256 * c : 256 * c + 256], found)
        answer[q] = found.astype(BF)

    def look_far(q, carry):
        look(q)
        ans_copy(q).start()
        return carry

    lax.fori_loop(1, 16, look_far, 0)
    look(0)
    permuted[0:16] = answer[0]
    to_blocks = jnp.where(lax.broadcasted_iota(jnp.int32, (128, 256), 1) == key_col, 1.0, 0.0).astype(BF)

    def take(q, carry):
        ans_arrival(q).wait_recv()
        permuted[pl.ds(pl.multiple_of(q * 16, 16), 16), :] = answered[q]
        return carry

    lax.fori_loop(1, 16, take, 0)
    values[...] = jnp.dot(to_blocks, permuted[...], preferred_element_type=F32)

    upper = lax.broadcasted_iota(jnp.int32, (8, 128), 0) < 4

    def at_pair(pair):
        return pl.ds(pl.multiple_of(8 * pair, 8), 8)

    def residual(pair, carry):
        at = at_pair(pair)
        both = lax.dot_general(values[at, :].astype(BF), phi_bf[pair], NT, preferred_element_type=F32)
        interp = jnp.where(upper, both[:, :128], both[:, 128:])
        resids[at, :] = held[at, :] * (goal[at, :] - interp)
        return carry

    def correction(pair, carry):
        at = at_pair(pair)
        both = lax.dot_general(resids[at, :].astype(BF), corr_bf[pair], NT, preferred_element_type=F32)
        values[at, 0:128] = jnp.where(upper, both[:, :128], 0.0)
        values[at, 128:256] = jnp.where(upper, 0.0, both[:, 128:])
        return carry

    def spreading(pair, carry):
        at = at_pair(pair)
        values[at, :] = jnp.dot(values[at, :].astype(BF), phi_bf[pair], preferred_element_type=F32)
        return carry

    lax.fori_loop(0, 16, residual, 0, unroll=8)
    lax.fori_loop(0, 16, correction, 0, unroll=8)
    lax.fori_loop(0, 16, spreading, 0, unroll=8)
    gives = jnp.dot(to_slots, values[...].astype(BF), preferred_element_type=F32).astype(BF)
    for q in range(16):
        giving[q] = gives[16 * q : 16 * q + 16]

    def start_give(q, carry):
        give_copy(q).start()
        return carry

    lax.fori_loop(1, 16, start_give, 0)
    given[0] = giving[0]

    def place(q):
        row, _ = spots(q)
        mask = rows_of == row
        amount = given[q].astype(F32)
        rows = []
        for i in range(3):
            line = jnp.concatenate([amount[4 * c + i : 4 * c + i + 1] for c in range(CAP)], axis=1)
            rows.append(jnp.where(mask, line, 0.0).astype(BF))
        return lax.dot_general(jnp.concatenate(rows, axis=0), hots[q], NT, preferred_element_type=F32)

    adding[...] = place(0)

    def place_far(q, carry):
        give_arrival(q).wait_recv()
        adding[...] += place(q)
        return carry

    lax.fori_loop(1, 16, place_far, 0)
    for i in range(3):
        part[i] = adding[128 * i : 128 * i + 128, :].astype(BF)

    def part_copy(step):
        theirs = pl.ds(pl.multiple_of(group_at(step) * 16, 16), 16)
        return pltpu.make_async_remote_copy(
            src_ref=part.at[:, theirs, :],
            dst_ref=got.at[24 + groups - step],
            send_sem=part_send.at[step],
            recv_sem=part_recv.at[groups - step],
            device_id=(slab, group_at(step)),
            device_id_type=MESH,
        )

    def part_arrival(step):
        theirs = pl.ds(pl.multiple_of(group_at(step) * 16, 16), 16)
        return pltpu.make_async_remote_copy(
            src_ref=part.at[:, theirs, :],
            dst_ref=got.at[24 + step],
            send_sem=part_send.at[step],
            recv_sem=part_recv.at[step],
            device_id=(slab, group_at(step)),
            device_id_type=MESH,
        )

    for step in range(1, groups):
        part_copy(step).start()
    share = jnp.stack([adding[pl.ds(pl.multiple_of(128 * i + group * 16, 16), 16), :] for i in range(3)])
    for step in range(1, groups):
        part_arrival(step).wait_recv()
        share = share + got[24 + step].astype(F32)
    halves[:, mine, :] = share.astype(BF)
    for step in range(1, groups):
        half_copy(step).start()
    for step in range(1, groups):
        half_arrival(step).wait_recv()
    for i in range(3):
        out[i] = state[i] + halves[i].astype(F32)

    def end_force(k, carry):
        force_copy(k).wait_send()
        return carry

    def end_far(q, carry):
        ask_copy(q).wait_send()
        ans_copy(q).wait_send()
        give_copy(q).wait_send()
        return carry

    def end_near(step, carry):
        sum_copy(step).wait_send()
        part_copy(step).wait_send()
        half_copy(step).wait_send()
        return carry

    to_above.wait_send()
    to_below.wait_send()
    lax.fori_loop(0, 23, end_force, 0)
    lax.fori_loop(1, 16, end_far, 0)
    lax.fori_loop(1, groups, end_near, 0)


def body(
    disp_now, disp_prev, inv_mass, cell_nodes, shape_grads, cell_weights, cell_shear, cell_bulk,
    block_owner, block_nodes, block_phi, block_corr, block_target, block_fixed,
):
    vmem = pl.BlockSpec(memory_space=pltpu.VMEM)
    anywhere = pl.BlockSpec(memory_space=pl.ANY)
    dma = pltpu.SemaphoreType.DMA
    message = pltpu.VMEM((16, 16, 256), BF)
    nodal = pltpu.VMEM((3, 128, 256), BF)
    result = pl.pallas_call(
        step_kernel,
        name="step",
        out_shape=jax.ShapeDtypeStruct((3, 128, 256), F32),
        in_specs=[anywhere] * 3 + [vmem, anywhere] + [vmem] * 5 + [anywhere] * 2 + [vmem] * 2,
        out_specs=vmem,
        scratch_shapes=[
            pltpu.VMEM((3, 32768), F32),
            pltpu.VMEM((3, 32768), F32),
            pltpu.VMEM((256, 128), F32),
            pltpu.VMEM((3, 128, 256), F32),
            pltpu.VMEM((3, 384, 256), BF),
            pltpu.VMEM((8, 1, QUAD), jnp.int32),
            pltpu.VMEM((32, 3, 192, 128), BF),
            pltpu.VMEM((3, 128, 128), F32),
            pltpu.VMEM((8, 8, QUAD), F32),
            pltpu.VMEM((8, 3, 256, QUAD), BF),
            pltpu.VMEM((8, 384, QUAD), BF),
            pltpu.VMEM((3, 3, 128, 256), BF),
            pltpu.VMEM((32, 3, 16, 256), BF),
            nodal,
            message, message, message, message, message, message,
            pltpu.VMEM((384, 256), F32),
            nodal,
            nodal,
            pltpu.VMEM((16, 256, 256), F32),
            pltpu.VMEM((16, 256, 128), F32),
            pltpu.VMEM((16, 256, 256), BF),
            pltpu.VMEM((16, 256, 128), BF),
            pltpu.VMEM((128, 128), F32),
            pltpu.VMEM((128, 128), F32),
            pltpu.VMEM((2, 128, 128), F32),
            pltpu.VMEM((128, 256), F32),
            pltpu.VMEM((128, 128), F32),
            pltpu.VMEM((256, 256), BF),
            pltpu.VMEM((384, 256), BF),
            pltpu.VMEM((16, 256, 1024), BF),
            dma((6,)), dma((3,)), dma((3,)), dma((23,)), dma((23,)), dma((8,)), dma((8,)), dma((16,)), dma((16,)),
            dma((16,)), dma((16,)), dma((16,)), dma((16,)), dma((8,)), dma((8,)), dma((8,)), dma((8,)),
        ],
        compiler_params=pltpu.CompilerParams(
            vmem_limit_bytes=58 << 20, collective_id=0, has_side_effects=True
        ),
    )(
        disp_now,
        disp_prev,
        inv_mass.reshape(256, 128),
        cell_nodes,
        shape_grads,
        cell_weights,
        cell_shear.reshape(1, 32),
        cell_bulk.reshape(1, 32),
        block_owner.reshape(1, 32),
        block_nodes,
        block_phi.reshape(16, 256, 256),
        block_corr.reshape(16, 256, 128),
        jnp.moveaxis(block_target, 1, 0),
        block_fixed,
    )
    return result.reshape(3, 32768)


def solution(mesh):
    both = ("slab", "group")
    placed = (
        P(None, "slab"), P(None, "slab"), P("slab"), P(both, None), P(both, None, None, None), P(both, None),
        P(both), P(both), P(both, None), P(both, None), P(both, None, None), P(both, None, None),
        P(both, None, None), P(both, None),
    )
    return jax.shard_map(body, mesh=mesh, in_specs=placed, out_specs=P(None, "slab"), check_vma=False)
```

time: 95.6 us -> 79.5 us (0.83)
  local copies, waits for them, and re-layouts: 10.1 us -> 2.06 us
  starting transfers between devices: 5.96 us -> 0 us
  other arithmetic: 2.01 us -> 0 us
    ppermute x2 -> x0, starting transfers between devices: 5.96 us -> none  [the longest x1 4.67 us: body(): low = lax.ppermute(own, 'slab', forward)]
    reshape x3 -> x0, local copies, waits for them, and re-layouts: 2.67 us -> none  [the longest x1 1.45 us: body(): cell_nodes.reshape(8, 1, QUAD)]
    broadcast_in_dim x2 -> x0, local copies, waits for them, and re-layouts: 2.67 us -> none  [the longest x1 1.33 us: body(): cell_shear[:, None]]
    unnamed x15 -> x1, local copies, waits for them, and re-layouts: 4.53 us -> 2.06 us
    convert_element_type x1 -> x0, other arithmetic: 1.13 us -> none  [body(): own = disp_now.astype(BF).reshape(384, 256)]
    pallas_call x2 -> x1, Pallas kernels: 76.9 us -> 76.8 us  [body(): pl.pallas_call(step_kernel, name='step', out_shape=jax.ShapeDtypeStruct((...]
  transfers between devices with their start and end apart: 2 -> 0, of which waited for: 0 -> 0; matrix products, arithmetic and copies ran while one was open for 8% -> 0% of each run, Pallas kernels for 0% -> 0%
where the time goes in v2:
time: 79.5 us; the launch traced here: 78.9 us
  Pallas kernels  76.8 us (97%)
  local copies, waits for them, and re-layouts  2.06 us (3%)
    pallas_call x1, Pallas kernels, body(): pl.pallas_call(step_kernel, name='step', out_shape=jax.ShapeDtypeStruct((...  76.8 us
    unnamed x1, local copies, waits for them, and re-layouts  2.06 us

profile of v2, /device:TPU:1, one launch (start us, length us, event | category | flops | bytes accessed | tf_op | source)
XLA Modules:
  0.0 78.9 jit_solution(2218762905011952596)
XLA Ops:
  0.0 76.8 %step.1 = f32[3,128,256]{2,1,0:T(8,128)} custom-call(f32[3,32768]{1,0:T(4,128)} %now_hbm.1, f32[3,32768]{1,0:T(4,128)} %prev_hbm.1, f32[256,128]{1,0:T(8,128)} %bitcast.12, s32[32,192]{1,0:T(8,128)} %cell_nodes.1, bf16[32,3,192,128]{3,2,1,0:T(8,128)(2,1)} %grads_hbm.1, f32[32,128]{1,0:T(8,128)} %weights.1, f32[1,32]{1,0:T(1,128)} %bitcast.14, ...), custom_call_target="tpu_custom_call" | custom-call | tf_op jit(solution)/shard_map/step/pallas_call | solution.py:533
  76.8 2.1 %copy.15 = f32[1,3,128,256]{3,1,2,0:T(4,128)} copy(f32[1,3,128,256]{3,2,1,0:T(8,128)} %bitcast.11) | data formatting | bytes 786432

commit v3 on v2

--- a/solution.py
+++ b/solution.py
@@ -21,10 +21,10 @@
 def step_kernel(
     now_hbm, prev_hbm, mass_hbm, cell_nodes, grads_hbm, weights, shear, bulk, owner, block_nodes, phi_hbm, corr_hbm,
     target, fixed, out,
-    lines, prev, mass, state, tables, nodes, grads, field, near, columns, spread, forces,
+    lines, prev, mass, state, tables, nodes, grads, field, near, columns, spread, forces, paired, merged,
     got, summed, asking, asked, answer, answered, giving, given, adding, part, halves,
     phi, corr, phi_bf, corr_bf, goal, held, numbers, values, resids, permuted, gathered, hots,
-    load_sem, halo_send, halo_recv, force_send, force_recv, all_send, all_recv, ask_send, ask_recv, ans_send, ans_recv,
+    load_sem, enter_sem, pair_send, pair_recv, halo_send, halo_recv, force_send, force_recv, all_send, all_recv, ask_send, ask_recv, ans_send, ans_recv,
     give_send, give_recv, part_send, part_recv, half_send, half_recv,
 ):
     slab, group = lax.axis_index("slab"), lax.axis_index("group")
@@ -33,8 +33,15 @@
     def slab_at(by):
         return lax.rem(slab + by + slabs, slabs)
 
-    def group_at(by):
-        return lax.rem(group + by + groups, groups)
+    depth, core = group // 2, lax.rem(group, 2)
+    depths = groups // 2
+    sibling = (slab, depth * 2 + 1 - core)
+
+    def depth_at(by):
+        return lax.rem(depth + by, depths)
+
+    def level(by):
+        return depth_at(by) * 2 + core
 
     load_now = pltpu.make_async_copy(now_hbm, lines, load_sem.at[0])
     load_grads = pltpu.make_async_copy(grads_hbm, grads, load_sem.at[1])
@@ -51,20 +58,17 @@
 
     barrier = pltpu.get_barrier_semaphore()
 
-    def near_device(k):
-        shift = jnp.where(k < 8, -1, jnp.where(k < 16, 1, 0))
-        return slab_at(shift), group_at(lax.rem(k + 1, groups))
-
-    def greet(k, carry):
-        pl.semaphore_signal(barrier, inc=1, device_id=near_device(k), device_id_type=MESH)
-        return carry
-
-    def greet_far(k, carry):
-        pl.semaphore_signal(barrier, inc=1, device_id=(slab_at(k), group), device_id_type=MESH)
-        return carry
-
-    lax.fori_loop(0, 23, greet, 0)
-    lax.fori_loop(2, 15, greet_far, 0)
+    def greet(device):
+        pl.semaphore_signal(barrier, inc=1, device_id=device, device_id_type=MESH)
+
+    def greet_again(device):
+        pl.semaphore_signal(enter_sem, inc=1, device_id=device, device_id_type=MESH)
+
+    for by in (1, 15, 4, 8, 12, 6, 10):
+        greet((slab_at(by), group))
+    for by in (1, 2, 3):
+        greet((slab, level(by)))
+    greet(sibling)
 
     def relaid(source, use):
         def move(block, carry):
@@ -84,7 +88,7 @@
     relaid(lines, set_state)
     for i in range(3):
         tables[1, 128 * i : 128 * i + 128, :] = state[i].astype(BF)
-    pl.semaphore_wait(barrier, 36)
+    pl.semaphore_wait(barrier, 11)
 
     def halo(side, by):
         return pltpu.make_async_remote_copy(
@@ -99,6 +103,10 @@
     to_above, to_below = halo(0, 1), halo(2, -1)
     to_above.start()
     to_below.start()
+    for by in (1, 15):
+        greet_again((slab_at(by), group))
+    for by in (1, 2, 3):
+        greet_again((slab, level(by)))
 
     own_row = owner[...]
     diag = lax.broadcasted_iota(jnp.int32, (32, 32), 0) == lax.broadcasted_iota(jnp.int32, (32, 32), 1)
@@ -157,7 +165,8 @@
         ask_copy(q).start()
         return carry
 
-    lax.fori_loop(1, 16, start_ask, 0)
+    pl.semaphore_wait(enter_sem, 5)
+    lax.fori_loop(1, 16, start_ask, 0, unroll=3)
     asked[0] = asking[0]
 
     def flatten(quad, carry):
@@ -184,7 +193,13 @@
             near[quad, i : i + 1, :] = line
         return carry
 
-    lax.fori_loop(0, 8, gather_own, 0)
+    lax.fori_loop(0, 8, gather_own, 0, unroll=2)
+    load_prev.wait()
+
+    def set_base(i, at, value):
+        state[i, at, :] = 2.0 * state[i, at, :] - value
+
+    relaid(prev, set_base)
     to_above.wait_recv()
     to_below.wait_recv()
     tables[0] = jnp.where(slab == 0, 0.0, tables[0].astype(F32)).astype(BF)
@@ -198,7 +213,7 @@
             near[quad, i : i + 1, :] += line
         return carry
 
-    lax.fori_loop(0, 8, gather_sides, 0)
+    lax.fori_loop(0, 8, gather_sides, 0, unroll=2)
     load_grads.wait()
     sub = lax.broadcasted_iota(jnp.int32, (8, 384), 0)
     lane = lax.broadcasted_iota(jnp.int32, (8, 384), 1)
@@ -217,7 +232,7 @@
                 field[j, at, :] = jnp.dot(left, both, preferred_element_type=F32)
         return carry
 
-    lax.fori_loop(0, 8, gradient, 0)
+    lax.fori_loop(0, 8, gradient, 0, unroll=2)
     full = [
         [field[j, pl.ds(i, 32, stride=4), :] + (1.0 if i == j else 0.0) for j in range(3)]
         for i in range(3)
@@ -258,39 +273,50 @@
                 spread[quad, 128 * i : 128 * i + 128, span] = jnp.where(mask, value, 0.0).astype(BF)
         return carry
 
-    lax.fori_loop(0, 8, cell_forces, 0)
+    lax.fori_loop(0, 8, cell_forces, 0, unroll=2)
+
+    def pair_copy(side):
+        return pltpu.make_async_remote_copy(
+            src_ref=forces.at[side, :, :, 1 - core],
+            dst_ref=paired.at[side],
+            send_sem=pair_send.at[side],
+            recv_sem=pair_recv.at[side],
+            device_id=sibling,
+            device_id_type=MESH,
+        )
 
     def force_copy(k):
-        source = jnp.where(k < 8, 0, jnp.where(k < 16, 2, 1))
-        start = pl.multiple_of(group_at(lax.rem(k + 1, groups)) * 16, 16)
+        source, shift, by = ((0, -1, k), (2, 1, k - 4), (1, 0, k - 7))[k // 4]
         return pltpu.make_async_remote_copy(
-            src_ref=forces.at[source, :, pl.ds(start, 16), :],
+            src_ref=merged.at[source, :, depth_at(by)],
             dst_ref=got.at[k],
             send_sem=force_send.at[k],
             recv_sem=force_recv.at[k],
-            device_id=near_device(k),
+            device_id=(slab_at(shift), level(by)),
             device_id_type=MESH,
         )
 
-    def start_force(k, carry):
-        force_copy(k).start()
-        return carry
-
-    for side, first, last in ((0, 0, 8), (2, 8, 16), (1, 16, 23)):
+    def scatter(side):
         total = None
         for quad in range(8):
             piece = lax.dot_general(spread[quad], columns[quad, side], NT, preferred_element_type=F32)
             total = piece if total is None else total + piece
         for i in range(3):
-            forces[side, i] = total[128 * i : 128 * i + 128].astype(BF)
-        lax.fori_loop(first, last, start_force, 0)
-
-    load_prev.wait()
-
-    def set_base(i, at, value):
-        state[i, at, :] = 2.0 * state[i, at, :] - value
-
-    relaid(prev, set_base)
+            forces[side, i] = total[128 * i : 128 * i + 128].reshape(4, 2, 16, 256).astype(BF)
+        pair_copy(side).start()
+
+    def merge(side, first, last):
+        pair_copy(side).wait_recv()
+        for i in range(3):
+            merged[side, i] = (forces[side, i, :, core].astype(F32) + paired[side, i].astype(F32)).astype(BF)
+        for k in range(first, last):
+            force_copy(k).start()
+
+    scatter(0)
+    scatter(2)
+    merge(0, 0, 4)
+    scatter(1)
+    merge(2, 4, 8)
 
     def spots(q):
         spot = asked[q].astype(F32)
@@ -307,7 +333,9 @@
         return carry
 
     heat(0)
-    lax.fori_loop(1, 16, heat_far, 0)
+    lax.fori_loop(1, 4, heat_far, 0, unroll=3)
+    merge(1, 8, 11)
+    lax.fori_loop(4, 16, heat_far, 0, unroll=3)
     for i in range(3):
         goal[pl.ds(i, 32, stride=4), :] = target[i]
     goal[pl.ds(3, 32, stride=4), :] = jnp.zeros((32, 128), F32)
@@ -324,51 +352,86 @@
     lax.fori_loop(0, 16, narrow, 0)
     load_mass.wait()
 
-    mine = pl.ds(pl.multiple_of(group * 16, 16), 16)
-    share = forces[1, :, mine, :].astype(F32)
-    for k in range(23):
+    share = merged[1, :, depth].astype(F32)
+    for k in range(11):
         force_copy(k).wait_recv()
         piece = got[k].astype(F32)
-        if k < 8:
+        if k < 4:
             piece = jnp.where(slab == slabs - 1, 0.0, piece)
-        elif k < 16:
+        elif k < 8:
             piece = jnp.where(slab == 0, 0.0, piece)
         share = share + piece
 
     def shared(buffer, send, recv):
-        def copy(step):
+        def copy(by):
             return pltpu.make_async_remote_copy(
-                src_ref=buffer.at[:, mine, :],
-                dst_ref=buffer.at[:, mine, :],
-                send_sem=send.at[step],
-                recv_sem=recv.at[groups - step],
-                device_id=(slab, group_at(step)),
+                src_ref=buffer.at[:, group],
+                dst_ref=buffer.at[:, group],
+                send_sem=send.at[by],
+                recv_sem=recv.at[depths - by],
+                device_id=(slab, level(by)),
                 device_id_type=MESH,
             )
 
-        def arrival(step):
-            theirs = pl.ds(pl.multiple_of(group_at(step) * 16, 16), 16)
+        def arrival(by):
             return pltpu.make_async_remote_copy(
-                src_ref=buffer.at[:, theirs, :],
-                dst_ref=buffer.at[:, theirs, :],
-                send_sem=send.at[step],
-                recv_sem=recv.at[step],
-                device_id=(slab, group_at(step)),
+                src_ref=buffer.at[:, level(by)],
+                dst_ref=buffer.at[:, level(by)],
+                send_sem=send.at[by],
+                recv_sem=recv.at[by],
+                device_id=(slab, level(by)),
                 device_id_type=MESH,
             )
 
-        return copy, arrival
-
-    sum_copy, sum_arrival = shared(summed, all_send, all_recv)
-    half_copy, half_arrival = shared(halves, half_send, half_recv)
-    summed[:, mine, :] = share.astype(BF)
-    for step in range(1, groups):
-        sum_copy(step).start()
+        def cross(by):
+            return pltpu.make_async_remote_copy(
+                src_ref=buffer.at[:, level(by)],
+                dst_ref=buffer.at[:, level(by)],
+                send_sem=send.at[depths + by],
+                recv_sem=recv.at[depths + by],
+                device_id=sibling,
+                device_id_type=MESH,
+            )
+
+        def crossed(by):
+            other = depth_at(by) * 2 + 1 - core
+            return pltpu.make_async_remote_copy(
+                src_ref=buffer.at[:, other],
+                dst_ref=buffer.at[:, other],
+                send_sem=send.at[depths + by],
+                recv_sem=recv.at[depths + by],
+                device_id=sibling,
+                device_id_type=MESH,
+            )
+
+        def begin():
+            for by in (2, 1, 3):
+                copy(by).start()
+            cross(0).start()
+
+        def finish():
+            for by in (1, 3, 2):
+                arrival(by).wait_recv()
+                cross(by).start()
+            for by in (0, 1, 3, 2):
+                crossed(by).wait_recv()
+
+        def close():
+            for by in (1, 2, 3):
+                copy(by).wait_send()
+            for by in range(4):
+                cross(by).wait_send()
+
+        return begin, finish, close
+
+    sum_begin, sum_finish, sum_close = shared(summed, all_send, all_recv)
+    half_begin, half_finish, half_close = shared(halves, half_send, half_recv)
+    summed[:, group] = share.astype(BF)
+    sum_begin()
     scale = jnp.concatenate([mass[pl.ds(0, 128, stride=2), :], mass[pl.ds(1, 128, stride=2), :]], axis=1)
-    for step in range(1, groups):
-        sum_arrival(step).wait_recv()
+    sum_finish()
     for i in range(3):
-        state[i] = state[i] - scale * summed[i].astype(F32)
+        state[i] = state[i] - scale * summed[i].reshape(128, 256).astype(F32)
         gathered[128 * i : 128 * i + 128, :] = state[i].astype(BF)
 
     rows_of = lax.broadcasted_iota(jnp.int32, (128, 1024), 0)
@@ -390,7 +453,7 @@
         ans_copy(q).start()
         return carry
 
-    lax.fori_loop(1, 16, look_far, 0)
+    lax.fori_loop(1, 16, look_far, 0, unroll=3)
     look(0)
     permuted[0:16] = answer[0]
     to_blocks = jnp.where(lax.broadcasted_iota(jnp.int32, (128, 256), 1) == key_col, 1.0, 0.0).astype(BF)
@@ -400,7 +463,7 @@
         permuted[pl.ds(pl.multiple_of(q * 16, 16), 16), :] = answered[q]
         return carry
 
-    lax.fori_loop(1, 16, take, 0)
+    lax.fori_loop(1, 16, take, 0, unroll=3)
     values[...] = jnp.dot(to_blocks, permuted[...], preferred_element_type=F32)
 
     upper = lax.broadcasted_iota(jnp.int32, (8, 128), 0) < 4
@@ -438,7 +501,7 @@
         give_copy(q).start()
         return carry
 
-    lax.fori_loop(1, 16, start_give, 0)
+    lax.fori_loop(1, 16, start_give, 0, unroll=3)
     given[0] = giving[0]
 
     def place(q):
@@ -453,54 +516,64 @@
 
     adding[...] = place(0)
 
-    def place_far(q, carry):
-        give_arrival(q).wait_recv()
-        adding[...] += place(q)
-        return carry
-
-    lax.fori_loop(1, 16, place_far, 0)
+    def place_far(third, carry):
+        total = None
+        for c in range(3):
+            q = 3 * third + 1 + c
+            give_arrival(q).wait_recv()
+            piece = place(q)
+            total = piece if total is None else total + piece
+        adding[...] += total
+        return carry
+
+    lax.fori_loop(0, 5, place_far, 0)
+
+    part_out = pltpu.make_async_remote_copy(
+        src_ref=part.at[:, :, 1 - core],
+        dst_ref=paired.at[3],
+        send_sem=pair_send.at[3],
+        recv_sem=pair_recv.at[3],
+        device_id=sibling,
+        device_id_type=MESH,
+    )
     for i in range(3):
-        part[i] = adding[128 * i : 128 * i + 128, :].astype(BF)
-
-    def part_copy(step):
-        theirs = pl.ds(pl.multiple_of(group_at(step) * 16, 16), 16)
+        part[i] = adding[128 * i : 128 * i + 128, :].reshape(4, 2, 16, 256).astype(BF)
+    part_out.start()
+
+    def part_copy(by):
         return pltpu.make_async_remote_copy(
-            src_ref=part.at[:, theirs, :],
-            dst_ref=got.at[24 + groups - step],
-            send_sem=part_send.at[step],
-            recv_sem=part_recv.at[groups - step],
-            device_id=(slab, group_at(step)),
+            src_ref=merged.at[3, :, depth_at(by)],
+            dst_ref=got.at[11 + depths - by],
+            send_sem=part_send.at[by],
+            recv_sem=part_recv.at[depths - by],
+            device_id=(slab, level(by)),
             device_id_type=MESH,
         )
 
-    def part_arrival(step):
-        theirs = pl.ds(pl.multiple_of(group_at(step) * 16, 16), 16)
+    def part_arrival(by):
         return pltpu.make_async_remote_copy(
-            src_ref=part.at[:, theirs, :],
-            dst_ref=got.at[24 + step],
-            send_sem=part_send.at[step],
-            recv_sem=part_recv.at[step],
-            device_id=(slab, group_at(step)),
+            src_ref=merged.at[3, :, depth_at(by)],
+            dst_ref=got.at[11 + by],
+            send_sem=part_send.at[by],
+            recv_sem=part_recv.at[by],
+            device_id=(slab, level(by)),
             device_id_type=MESH,
         )
 
-    for step in range(1, groups):
-        part_copy(step).start()
-    share = jnp.stack([adding[pl.ds(pl.multiple_of(128 * i + group * 16, 16), 16), :] for i in range(3)])
-    for step in range(1, groups):
-        part_arrival(step).wait_recv()
-        share = share + got[24 + step].astype(F32)
-    halves[:, mine, :] = share.astype(BF)
-    for step in range(1, groups):
-        half_copy(step).start()
-    for step in range(1, groups):
-        half_arrival(step).wait_recv()
+    part_out.wait_recv()
     for i in range(3):
-        out[i] = state[i] + halves[i].astype(F32)
-
-    def end_force(k, carry):
-        force_copy(k).wait_send()
-        return carry
+        merged[3, i] = (part[i, :, core].astype(F32) + paired[3, i].astype(F32)).astype(BF)
+    for by in (2, 1, 3):
+        part_copy(by).start()
+    share = merged[3, :, depth].astype(F32)
+    for by in (1, 3, 2):
+        part_arrival(by).wait_recv()
+        share = share + got[11 + by].astype(F32)
+    halves[:, group] = share.astype(BF)
+    half_begin()
+    half_finish()
+    for i in range(3):
+        out[i] = state[i] + halves[i].reshape(128, 256).astype(F32)
 
     def end_far(q, carry):
         ask_copy(q).wait_send()
@@ -508,17 +581,18 @@
         give_copy(q).wait_send()
         return carry
 
-    def end_near(step, carry):
-        sum_copy(step).wait_send()
-        part_copy(step).wait_send()
-        half_copy(step).wait_send()
-        return carry
-
     to_above.wait_send()
     to_below.wait_send()
-    lax.fori_loop(0, 23, end_force, 0)
+    for side in range(3):
+        pair_copy(side).wait_send()
+    for k in range(11):
+        force_copy(k).wait_send()
     lax.fori_loop(1, 16, end_far, 0)
-    lax.fori_loop(1, groups, end_near, 0)
+    sum_close()
+    part_out.wait_send()
+    for by in (1, 2, 3):
+        part_copy(by).wait_send()
+    half_close()
 
 
 def body(
@@ -529,7 +603,8 @@
     anywhere = pl.BlockSpec(memory_space=pl.ANY)
     dma = pltpu.SemaphoreType.DMA
     message = pltpu.VMEM((16, 16, 256), BF)
-    nodal = pltpu.VMEM((3, 128, 256), BF)
+    nodal = pltpu.VMEM((3, 8, 16, 256), BF)
+    paired = pltpu.VMEM((4, 3, 4, 16, 256), BF)
     result = pl.pallas_call(
         step_kernel,
         name="step",
@@ -548,12 +623,14 @@
             pltpu.VMEM((8, 8, QUAD), F32),
             pltpu.VMEM((8, 3, 256, QUAD), BF),
             pltpu.VMEM((8, 384, QUAD), BF),
-            pltpu.VMEM((3, 3, 128, 256), BF),
-            pltpu.VMEM((32, 3, 16, 256), BF),
+            pltpu.VMEM((3, 3, 4, 2, 16, 256), BF),
+            paired,
+            paired,
+            pltpu.VMEM((15, 3, 16, 256), BF),
             nodal,
             message, message, message, message, message, message,
             pltpu.VMEM((384, 256), F32),
-            nodal,
+            pltpu.VMEM((3, 4, 2, 16, 256), BF),
             nodal,
             pltpu.VMEM((16, 256, 256), F32),
             pltpu.VMEM((16, 256, 128), F32),
@@ -567,11 +644,12 @@
             pltpu.VMEM((256, 256), BF),
             pltpu.VMEM((384, 256), BF),
             pltpu.VMEM((16, 256, 1024), BF),
-            dma((6,)), dma((3,)), dma((3,)), dma((23,)), dma((23,)), dma((8,)), dma((8,)), dma((16,)), dma((16,)),
-            dma((16,)), dma((16,)), dma((16,)), dma((16,)), dma((8,)), dma((8,)), dma((8,)), dma((8,)),
+            dma((6,)), pltpu.SemaphoreType.REGULAR, dma((4,)), dma((4,)), dma((3,)), dma((3,)), dma((11,)), dma((11,)),
+            dma((8,)), dma((8,)), dma((16,)), dma((16,)), dma((16,)), dma((16,)), dma((16,)), dma((16,)), dma((4,)),
+            dma((4,)), dma((8,)), dma((8,)),
         ],
         compiler_params=pltpu.CompilerParams(
-            vmem_limit_bytes=58 << 20, collective_id=0, has_side_effects=True
+            vmem_limit_bytes=46 << 20, collective_id=0, has_side_effects=True
         ),
     )(
         disp_now,

time: 79.5 us -> 89.4 us (1.12)
  local copies, waits for them, and re-layouts: 2.06 us -> 13.5 us
  Pallas kernels: 76.8 us -> 75.2 us
    unnamed x1 -> x27, local copies, waits for them, and re-layouts: 2.06 us -> 13.5 us
    pallas_call x1, Pallas kernels: 76.8 us -> 75.2 us  [body(): pl.pallas_call(step_kernel, name='step', out_shape=jax.ShapeDtypeStruct((...]
where the time goes in v3:
time: 89.4 us; the launch traced here: 88.8 us
  Pallas kernels  75.2 us (84%)
  local copies, waits for them, and re-layouts  13.5 us (15%)
    pallas_call x1, Pallas kernels, body(): pl.pallas_call(step_kernel, name='step', out_shape=jax.ShapeDtypeStruct((...  75.2 us
    unnamed x27, local copies, waits for them, and re-layouts  13.5 us

profile of v3, /device:TPU:1, one launch (start us, length us, event | category | flops | bytes accessed | tf_op | source)
XLA Modules:
  0.0 88.8 jit_solution(3474878855854600079)
XLA Ops:
  0.0 0.0 copy-start
  0.0 2.2 %copy-done = f32[32,128,256]{2,1,0:T(8,128)S(1)} copy-done((f32[32,128,256]{2,1,0:T(8,128)S(1)}, f32[32,128,256]{2,1,0:T(8,128)}, u32[]{:S(2)}) %copy-start) | copy-done | bytes 4194328
  2.2 0.0 copy-start.1
  2.2 1.6 %copy-done.1 = f32[32,128,128]{2,1,0:T(8,128)S(1)} copy-done((f32[32,128,128]{2,1,0:T(8,128)S(1)}, f32[32,128,128]{2,1,0:T(8,128)}, u32[]{:S(2)}) %copy-start.1) | copy-done | bytes 2097176
  3.8 0.0 copy-start.2
  3.8 1.0 %copy-done.2 = f32[3,32768]{1,0:T(4,128)S(1)} copy-done((f32[3,32768]{1,0:T(4,128)S(1)}, f32[3,32768]{1,0:T(4,128)}, u32[]{:S(2)}) %copy-start.2) | copy-done | bytes 393240
  4.8 0.0 copy-start.3
  4.8 1.0 %copy-done.3 = f32[3,32768]{1,0:T(4,128)S(1)} copy-done((f32[3,32768]{1,0:T(4,128)S(1)}, f32[3,32768]{1,0:T(4,128)}, u32[]{:S(2)}) %copy-start.3) | copy-done | bytes 393240
  5.9 0.0 copy-start.4
  5.9 0.9 %copy-done.4 = f32[32768]{0:T(1024)S(1)} copy-done((f32[32768]{0:T(1024)S(1)}, f32[32768]{0:T(1024)}, u32[]{:S(2)}) %copy-start.4) | copy-done | bytes 131096
  6.8 0.0 copy-start.5
  6.8 0.8 copy-done.5
  7.6 0.0 copy-start.6
  7.6 0.8 copy-done.6
  8.3 0.0 copy-start.7
  8.3 0.8 copy-done.7
  9.1 0.0 copy-start.8
  9.1 0.7 copy-done.8
  9.8 0.0 copy-start.9
  9.8 0.7 copy-done.9
  10.5 0.0 copy-start.10
  10.5 0.7 copy-done.10
  11.2 0.0 copy-start.11
  11.2 0.7 copy-done.11
  11.8 0.0 copy-start.12
  11.8 0.7 copy-done.12
  12.5 75.2 %step.1 = f32[3,128,256]{2,1,0:T(8,128)S(1)} custom-call(f32[3,32768]{1,0:T(4,128)S(1)} %copy-done.2, f32[3,32768]{1,0:T(4,128)S(1)} %copy-done.3, f32[256,128]{1,0:T(8,128)S(1)} %bitcast.12, s32[32,192]{1,0:T(8,128)S(1)} %copy-done.6, bf16[32,3,192,128]{3,2,1,0:T(8,128)(2,1)} %grads_hbm.1, f32[32,128]{1,0:T(8,128)S(1)} %copy-done.8, f32[1,32]{1,0:T(1,128)S(1)} %bitcast.14, ...), custom_call_target="tpu_custom_call" | custom-call | tf_op jit(solution)/shard_map/step/pallas_call | solution.py:608
  87.7 1.1 %copy.15 = f32[1,3,128,256]{3,1,2,0:T(4,128)} copy(f32[1,3,128,256]{3,2,1,0:T(8,128)S(1)} %bitcast.11) | data formatting | bytes 786432
Async XLA Ops:
  0.0 2.2 %copy-start = (f32[32,128,256]{2,1,0:T(8,128)S(1)}, f32[32,128,256]{2,1,0:T(8,128)}, u32[]{:S(2)}) copy-start(f32[32,128,256]{2,1,0:T(8,128)} %param.24) | copy-start | bytes 12582916
  2.2 1.6 %copy-start.1 = (f32[32,128,128]{2,1,0:T(8,128)S(1)}, f32[32,128,128]{2,1,0:T(8,128)}, u32[]{:S(2)}) copy-start(f32[32,128,128]{2,1,0:T(8,128)} %param.25) | copy-start | bytes 6291460
  3.8 1.0 %copy-start.2 = (f32[3,32768]{1,0:T(4,128)S(1)}, f32[3,32768]{1,0:T(4,128)}, u32[]{:S(2)}) copy-start(f32[3,32768]{1,0:T(4,128)} %now_hbm.1) | copy-start | bytes 1179652
  4.8 1.0 %copy-start.3 = (f32[3,32768]{1,0:T(4,128)S(1)}, f32[3,32768]{1,0:T(4,128)}, u32[]{:S(2)}) copy-start(f32[3,32768]{1,0:T(4,128)} %prev_hbm.1) | copy-start | bytes 1179652
  5.9 0.9 %copy-start.4 = (f32[32768]{0:T(1024)S(1)}, f32[32768]{0:T(1024)}, u32[]{:S(2)}) copy-start(f32[32768]{0:T(1024)} %param.16) | copy-start | bytes 393220
  6.8 0.8 copy-start.5
  7.6 0.8 copy-start.6
  8.3 0.8 copy-start.7
  9.1 0.7 copy-start.8
  9.8 0.7 copy-start.9
  10.5 0.7 copy-start.10
  11.2 0.7 copy-start.11
  11.8 0.7 copy-start.12

commit v4 on v3

--- a/solution.py
+++ b/solution.py
@@ -11,6 +11,8 @@
 MESH = pl.DeviceIdType.MESH
 CAP = 4
 QUAD = 768
+FAR = tuple(range(1, 16))
+NEAR = FAR
 
 
 def onehot(index, size):
@@ -21,9 +23,9 @@
 def step_kernel(
     now_hbm, prev_hbm, mass_hbm, cell_nodes, grads_hbm, weights, shear, bulk, owner, block_nodes, phi_hbm, corr_hbm,
     target, fixed, out,
-    lines, prev, mass, state, tables, nodes, grads, field, near, columns, spread, forces, paired, merged,
+    lines, prev, mass, state, tables, nodes, grads, field, near, columns, spread, forces, paired, merged, pooled,
     got, summed, asking, asked, answer, answered, giving, given, adding, part, halves,
-    phi, corr, phi_bf, corr_bf, goal, held, numbers, values, resids, permuted, gathered, hots,
+    phi, corr, phi_bf, corr_bf, goal, held, numbers, values, resids, gathered, hots,
     load_sem, enter_sem, pair_send, pair_recv, halo_send, halo_recv, force_send, force_recv, all_send, all_recv, ask_send, ask_recv, ans_send, ans_recv,
     give_send, give_recv, part_send, part_recv, half_send, half_recv,
 ):
@@ -42,6 +44,9 @@
 
     def level(by):
         return depth_at(by) * 2 + core
+
+    def group_at(by):
+        return lax.rem(group + by, groups)
 
     load_now = pltpu.make_async_copy(now_hbm, lines, load_sem.at[0])
     load_grads = pltpu.make_async_copy(grads_hbm, grads, load_sem.at[1])
@@ -101,8 +106,9 @@
         )
 
     to_above, to_below = halo(0, 1), halo(2, -1)
-    to_above.start()
-    to_below.start()
+    has_below, has_above = slab > 0, slab < slabs - 1
+    pl.when(has_above)(to_above.start)
+    pl.when(has_below)(to_below.start)
     for by in (1, 15):
         greet_again((slab_at(by), group))
     for by in (1, 2, 3):
@@ -131,8 +137,7 @@
         numbers[side, pl.ds(1, 32, stride=4), :] = ((node[:, span] & 255) + 1).astype(F32)
     named = jnp.concatenate([numbers[0], numbers[1]], axis=1).astype(BF)
     asks = jnp.dot(to_slots, named, preferred_element_type=F32) - 1.0
-    for q in range(16):
-        asking[q] = asks[16 * q : 16 * q + 16].astype(BF)
+    asking[...] = asks.astype(BF).reshape(16, 16, 256)
 
     def exchange(source, landing, send, recv):
         def copy(q):
@@ -157,16 +162,19 @@
 
         return copy, arrival
 
+    def ordered(order, turn, c):
+        q = order[c]
+        for t in range(1, 3):
+            q = jnp.where(turn == t, order[5 * t + c], q)
+        return q
+
     ask_copy, ask_arrival = exchange(asking, asked, ask_send, ask_recv)
     ans_copy, ans_arrival = exchange(answer, answered, ans_send, ans_recv)
     give_copy, give_arrival = exchange(giving, given, give_send, give_recv)
 
-    def start_ask(q, carry):
+    pl.semaphore_wait(enter_sem, 5)
+    for q in FAR:
         ask_copy(q).start()
-        return carry
-
-    pl.semaphore_wait(enter_sem, 5)
-    lax.fori_loop(1, 16, start_ask, 0, unroll=3)
     asked[0] = asking[0]
 
     def flatten(quad, carry):
@@ -200,10 +208,13 @@
         state[i, at, :] = 2.0 * state[i, at, :] - value
 
     relaid(prev, set_base)
-    to_above.wait_recv()
-    to_below.wait_recv()
-    tables[0] = jnp.where(slab == 0, 0.0, tables[0].astype(F32)).astype(BF)
-    tables[2] = jnp.where(slab == slabs - 1, 0.0, tables[2].astype(F32)).astype(BF)
+    def absent(side):
+        tables[side] = jnp.zeros((384, 256), BF)
+
+    pl.when(has_below)(to_above.wait_recv)
+    pl.when(has_above)(to_below.wait_recv)
+    pl.when(slab == 0)(lambda: absent(0))
+    pl.when(slab == slabs - 1)(lambda: absent(2))
 
     def gather_sides(quad, carry):
         row = (nodes[quad] >> 8) & 127
@@ -213,7 +224,7 @@
             near[quad, i : i + 1, :] += line
         return carry
 
-    lax.fori_loop(0, 8, gather_sides, 0, unroll=2)
+    lax.fori_loop(0, 8, gather_sides, 0, unroll=4)
     load_grads.wait()
     sub = lax.broadcasted_iota(jnp.int32, (8, 384), 0)
     lane = lax.broadcasted_iota(jnp.int32, (8, 384), 1)
@@ -232,7 +243,7 @@
                 field[j, at, :] = jnp.dot(left, both, preferred_element_type=F32)
         return carry
 
-    lax.fori_loop(0, 8, gradient, 0, unroll=2)
+    lax.fori_loop(0, 8, gradient, 0, unroll=4)
     full = [
         [field[j, pl.ds(i, 32, stride=4), :] + (1.0 if i == j else 0.0) for j in range(3)]
         for i in range(3)
@@ -273,7 +284,7 @@
                 spread[quad, 128 * i : 128 * i + 128, span] = jnp.where(mask, value, 0.0).astype(BF)
         return carry
 
-    lax.fori_loop(0, 8, cell_forces, 0, unroll=2)
+    lax.fori_loop(0, 8, cell_forces, 0, unroll=4)
 
     def pair_copy(side):
         return pltpu.make_async_remote_copy(
@@ -309,8 +320,11 @@
         pair_copy(side).wait_recv()
         for i in range(3):
             merged[side, i] = (forces[side, i, :, core].astype(F32) + paired[side, i].astype(F32)).astype(BF)
-        for k in range(first, last):
-            force_copy(k).start()
+        def leave():
+            for k in range(first, last):
+                force_copy(k).start()
+
+        pl.when((has_below, slab >= 0, has_above)[side])(leave)
 
     scatter(0)
     scatter(2)
@@ -333,9 +347,8 @@
         return carry
 
     heat(0)
-    lax.fori_loop(1, 4, heat_far, 0, unroll=3)
     merge(1, 8, 11)
-    lax.fori_loop(4, 16, heat_far, 0, unroll=3)
+    lax.fori_loop(1, 16, heat_far, 0, unroll=3)
     for i in range(3):
         goal[pl.ds(i, 32, stride=4), :] = target[i]
     goal[pl.ds(3, 32, stride=4), :] = jnp.zeros((32, 128), F32)
@@ -352,15 +365,18 @@
     lax.fori_loop(0, 16, narrow, 0)
     load_mass.wait()
 
-    share = merged[1, :, depth].astype(F32)
-    for k in range(11):
-        force_copy(k).wait_recv()
-        piece = got[k].astype(F32)
-        if k < 4:
-            piece = jnp.where(slab == slabs - 1, 0.0, piece)
-        elif k < 8:
-            piece = jnp.where(slab == 0, 0.0, piece)
-        share = share + piece
+    pooled[...] = merged[1, :, depth].astype(F32)
+
+    def collect(first, last):
+        value = pooled[...]
+        for k in range(first, last):
+            force_copy(k).wait_recv()
+            value = value + got[k].astype(F32)
+        pooled[...] = value
+
+    collect(8, 11)
+    pl.when(has_above)(lambda: collect(0, 4))
+    pl.when(has_below)(lambda: collect(4, 8))
 
     def shared(buffer, send, recv):
         def copy(by):
@@ -368,65 +384,38 @@
                 src_ref=buffer.at[:, group],
                 dst_ref=buffer.at[:, group],
                 send_sem=send.at[by],
-                recv_sem=recv.at[depths - by],
-                device_id=(slab, level(by)),
+                recv_sem=recv.at[groups - by],
+                device_id=(slab, group_at(by)),
                 device_id_type=MESH,
             )
 
         def arrival(by):
             return pltpu.make_async_remote_copy(
-                src_ref=buffer.at[:, level(by)],
-                dst_ref=buffer.at[:, level(by)],
+                src_ref=buffer.at[:, group_at(by)],
+                dst_ref=buffer.at[:, group_at(by)],
                 send_sem=send.at[by],
                 recv_sem=recv.at[by],
-                device_id=(slab, level(by)),
+                device_id=(slab, group_at(by)),
                 device_id_type=MESH,
             )
 
-        def cross(by):
-            return pltpu.make_async_remote_copy(
-                src_ref=buffer.at[:, level(by)],
-                dst_ref=buffer.at[:, level(by)],
-                send_sem=send.at[depths + by],
-                recv_sem=recv.at[depths + by],
-                device_id=sibling,
-                device_id_type=MESH,
-            )
-
-        def crossed(by):
-            other = depth_at(by) * 2 + 1 - core
-            return pltpu.make_async_remote_copy(
-                src_ref=buffer.at[:, other],
-                dst_ref=buffer.at[:, other],
-                send_sem=send.at[depths + by],
-                recv_sem=recv.at[depths + by],
-                device_id=sibling,
-                device_id_type=MESH,
-            )
-
         def begin():
-            for by in (2, 1, 3):
+            for by in (4, 3, 5, 2, 6, 1, 7):
                 copy(by).start()
-            cross(0).start()
 
         def finish():
-            for by in (1, 3, 2):
+            for by in (1, 7, 2, 6, 3, 5, 4):
                 arrival(by).wait_recv()
-                cross(by).start()
-            for by in (0, 1, 3, 2):
-                crossed(by).wait_recv()
 
         def close():
-            for by in (1, 2, 3):
+            for by in range(1, groups):
                 copy(by).wait_send()
-            for by in range(4):
-                cross(by).wait_send()
 
         return begin, finish, close
 
     sum_begin, sum_finish, sum_close = shared(summed, all_send, all_recv)
     half_begin, half_finish, half_close = shared(halves, half_send, half_recv)
-    summed[:, group] = share.astype(BF)
+    summed[:, group] = pooled[...].astype(BF)
     sum_begin()
     scale = jnp.concatenate([mass[pl.ds(0, 128, stride=2), :], mass[pl.ds(1, 128, stride=2), :]], axis=1)
     sum_finish()
@@ -446,25 +435,22 @@
             line = jnp.sum(jnp.where(mask, hit[128 * i : 128 * i + 128], 0.0), axis=0, keepdims=True)
             for c in range(CAP):
                 found = jnp.where(sixteen == 4 * c + i, line[:, 256 * c : 256 * c + 256], found)
-        answer[q] = found.astype(BF)
-
-    def look_far(q, carry):
-        look(q)
-        ans_copy(q).start()
-        return carry
-
-    lax.fori_loop(1, 16, look_far, 0, unroll=3)
-    look(0)
-    permuted[0:16] = answer[0]
+        return found.astype(BF)
+
+    def look_far(turn, carry):
+        for c in range(5):
+            q = ordered(FAR, turn, c)
+            answer[q] = look(q)
+            ans_copy(q).start()
+        return carry
+
+    lax.fori_loop(0, 3, look_far, 0)
+    answered[0] = look(0)
     to_blocks = jnp.where(lax.broadcasted_iota(jnp.int32, (128, 256), 1) == key_col, 1.0, 0.0).astype(BF)
 
-    def take(q, carry):
+    for q in NEAR:
         ans_arrival(q).wait_recv()
-        permuted[pl.ds(pl.multiple_of(q * 16, 16), 16), :] = answered[q]
-        return carry
-
-    lax.fori_loop(1, 16, take, 0, unroll=3)
-    values[...] = jnp.dot(to_blocks, permuted[...], preferred_element_type=F32)
+    values[...] = jnp.dot(to_blocks, answered[...].reshape(256, 256), preferred_element_type=F32)
 
     upper = lax.broadcasted_iota(jnp.int32, (8, 128), 0) < 4
 
@@ -494,14 +480,9 @@
     lax.fori_loop(0, 16, correction, 0, unroll=8)
     lax.fori_loop(0, 16, spreading, 0, unroll=8)
     gives = jnp.dot(to_slots, values[...].astype(BF), preferred_element_type=F32).astype(BF)
-    for q in range(16):
-        giving[q] = gives[16 * q : 16 * q + 16]
-
-    def start_give(q, carry):
+    giving[...] = gives.reshape(16, 16, 256)
+    for q in FAR:
         give_copy(q).start()
-        return carry
-
-    lax.fori_loop(1, 16, start_give, 0, unroll=3)
     given[0] = giving[0]
 
     def place(q):
@@ -516,57 +497,44 @@
 
     adding[...] = place(0)
 
-    def place_far(third, carry):
+    def place_far(turn, carry):
         total = None
-        for c in range(3):
-            q = 3 * third + 1 + c
+        for c in range(5):
+            q = ordered(NEAR, turn, c)
             give_arrival(q).wait_recv()
             piece = place(q)
             total = piece if total is None else total + piece
         adding[...] += total
         return carry
 
-    lax.fori_loop(0, 5, place_far, 0)
-
-    part_out = pltpu.make_async_remote_copy(
-        src_ref=part.at[:, :, 1 - core],
-        dst_ref=paired.at[3],
-        send_sem=pair_send.at[3],
-        recv_sem=pair_recv.at[3],
-        device_id=sibling,
-        device_id_type=MESH,
-    )
+    lax.fori_loop(0, 3, place_far, 0)
     for i in range(3):
-        part[i] = adding[128 * i : 128 * i + 128, :].reshape(4, 2, 16, 256).astype(BF)
-    part_out.start()
+        part[i] = adding[128 * i : 128 * i + 128, :].reshape(8, 16, 256).astype(BF)
 
     def part_copy(by):
         return pltpu.make_async_remote_copy(
-            src_ref=merged.at[3, :, depth_at(by)],
-            dst_ref=got.at[11 + depths - by],
+            src_ref=part.at[:, group_at(by)],
+            dst_ref=got.at[11 + groups - by],
             send_sem=part_send.at[by],
-            recv_sem=part_recv.at[depths - by],
-            device_id=(slab, level(by)),
+            recv_sem=part_recv.at[groups - by],
+            device_id=(slab, group_at(by)),
             device_id_type=MESH,
         )
 
     def part_arrival(by):
         return pltpu.make_async_remote_copy(
-            src_ref=merged.at[3, :, depth_at(by)],
+            src_ref=part.at[:, group_at(by)],
             dst_ref=got.at[11 + by],
             send_sem=part_send.at[by],
             recv_sem=part_recv.at[by],
-            device_id=(slab, level(by)),
+            device_id=(slab, group_at(by)),
             device_id_type=MESH,
         )
 
-    part_out.wait_recv()
-    for i in range(3):
-        merged[3, i] = (part[i, :, core].astype(F32) + paired[3, i].astype(F32)).astype(BF)
-    for by in (2, 1, 3):
+    for by in (4, 3, 5, 2, 6, 1, 7):
         part_copy(by).start()
-    share = merged[3, :, depth].astype(F32)
-    for by in (1, 3, 2):
+    share = part[:, group].astype(F32)
+    for by in (1, 7, 2, 6, 3, 5, 4):
         part_arrival(by).wait_recv()
         share = share + got[11 + by].astype(F32)
     halves[:, group] = share.astype(BF)
@@ -581,16 +549,20 @@
         give_copy(q).wait_send()
         return carry
 
-    to_above.wait_send()
-    to_below.wait_send()
+    pl.when(has_above)(to_above.wait_send)
+    pl.when(has_below)(to_below.wait_send)
     for side in range(3):
         pair_copy(side).wait_send()
-    for k in range(11):
-        force_copy(k).wait_send()
+    def sent(first, last):
+        for k in range(first, last):
+            force_copy(k).wait_send()
+
+    pl.when(has_below)(lambda: sent(0, 4))
+    pl.when(has_above)(lambda: sent(4, 8))
+    sent(8, 11)
     lax.fori_loop(1, 16, end_far, 0)
     sum_close()
-    part_out.wait_send()
-    for by in (1, 2, 3):
+    for by in range(1, groups):
         part_copy(by).wait_send()
     half_close()
 
@@ -604,7 +576,7 @@
     dma = pltpu.SemaphoreType.DMA
     message = pltpu.VMEM((16, 16, 256), BF)
     nodal = pltpu.VMEM((3, 8, 16, 256), BF)
-    paired = pltpu.VMEM((4, 3, 4, 16, 256), BF)
+    paired = pltpu.VMEM((3, 3, 4, 16, 256), BF)
     result = pl.pallas_call(
         step_kernel,
         name="step",
@@ -626,11 +598,12 @@
             pltpu.VMEM((3, 3, 4, 2, 16, 256), BF),
             paired,
             paired,
-            pltpu.VMEM((15, 3, 16, 256), BF),
+            pltpu.VMEM((3, 16, 256), F32),
+            pltpu.VMEM((19, 3, 16, 256), BF),
             nodal,
             message, message, message, message, message, message,
             pltpu.VMEM((384, 256), F32),
-            pltpu.VMEM((3, 4, 2, 16, 256), BF),
+            nodal,
             nodal,
             pltpu.VMEM((16, 256, 256), F32),
             pltpu.VMEM((16, 256, 128), F32),
@@ -641,15 +614,14 @@
             pltpu.VMEM((2, 128, 128), F32),
             pltpu.VMEM((128, 256), F32),
             pltpu.VMEM((128, 128), F32),
-            pltpu.VMEM((256, 256), BF),
             pltpu.VMEM((384, 256), BF),
             pltpu.VMEM((16, 256, 1024), BF),
-            dma((6,)), pltpu.SemaphoreType.REGULAR, dma((4,)), dma((4,)), dma((3,)), dma((3,)), dma((11,)), dma((11,)),
-            dma((8,)), dma((8,)), dma((16,)), dma((16,)), dma((16,)), dma((16,)), dma((16,)), dma((16,)), dma((4,)),
-            dma((4,)), dma((8,)), dma((8,)),
+            dma((6,)), pltpu.SemaphoreType.REGULAR, dma((3,)), dma((3,)), dma((3,)), dma((3,)), dma((11,)), dma((11,)),
+            dma((8,)), dma((8,)), dma((16,)), dma((16,)), dma((16,)), dma((16,)), dma((16,)), dma((16,)), dma((8,)),
+            dma((8,)), dma((8,)), dma((8,)),
         ],
         compiler_params=pltpu.CompilerParams(
-            vmem_limit_bytes=46 << 20, collective_id=0, has_side_effects=True
+            vmem_limit_bytes=60 << 20, collective_id=0, has_side_effects=True
         ),
     )(
         disp_now,

time: 89.4 us -> 77 us (0.86)
  local copies, waits for them, and re-layouts: 13.5 us -> 2.06 us
    unnamed x27 -> x1, local copies, waits for them, and re-layouts: 13.5 us -> 2.06 us
where the time goes in v4:
time: 77 us; the launch traced here: 76.8 us
  Pallas kernels  74.7 us (97%)
  local copies, waits for them, and re-layouts  2.06 us (3%)
    pallas_call x1, Pallas kernels, body(): pl.pallas_call(step_kernel, name='step', out_shape=jax.ShapeDtypeStruct((...  74.7 us
    unnamed x1, local copies, waits for them, and re-layouts  2.06 us

profile of v4, /device:TPU:1, one launch (start us, length us, event | category | flops | bytes accessed | tf_op | source)
XLA Modules:
  0.0 76.8 jit_solution(14367670103704467684)
XLA Ops:
  0.0 74.7 %step.1 = f32[3,128,256]{2,1,0:T(8,128)} custom-call(f32[3,32768]{1,0:T(4,128)} %now_hbm.1, f32[3,32768]{1,0:T(4,128)} %prev_hbm.1, f32[256,128]{1,0:T(8,128)} %bitcast.12, s32[32,192]{1,0:T(8,128)} %cell_nodes.1, bf16[32,3,192,128]{3,2,1,0:T(8,128)(2,1)} %grads_hbm.1, f32[32,128]{1,0:T(8,128)} %weights.1, f32[1,32]{1,0:T(1,128)} %bitcast.14, ...), custom_call_target="tpu_custom_call" | custom-call | tf_op jit(solution)/shard_map/step/pallas_call | solution.py:580
  74.7 2.1 %copy.15 = f32[1,3,128,256]{3,1,2,0:T(4,128)} copy(f32[1,3,128,256]{3,2,1,0:T(8,128)} %bitcast.11) | data formatting | bytes 786432

commit v5 on v4

--- a/solution.py
+++ b/solution.py
@@ -21,8 +21,9 @@
 
 
 def step_kernel(
-    now_hbm, prev_hbm, mass_hbm, cell_nodes, grads_hbm, weights, shear, bulk, owner, block_nodes, phi_hbm, corr_hbm,
-    target, fixed, out,
+    now_hbm, prev_hbm, mass_hbm, cell_nodes_hbm, grads_hbm, weights_hbm, shear_hbm, bulk_hbm, owner_hbm, block_nodes_hbm,
+    phi_hbm, corr_hbm, target_hbm, fixed_hbm, out,
+    cell_nodes, weights, shear, bulk, owner, block_nodes, target, fixed,
     lines, prev, mass, state, tables, nodes, grads, field, near, columns, spread, forces, paired, merged, pooled,
     got, summed, asking, asked, answer, answered, giving, given, adding, part, halves,
     phi, corr, phi_bf, corr_bf, goal, held, numbers, values, resids, gathered, hots,
@@ -54,7 +55,18 @@
     load_mass = pltpu.make_async_copy(mass_hbm, mass, load_sem.at[3])
     load_phi = pltpu.make_async_copy(phi_hbm, phi, load_sem.at[4])
     load_corr = pltpu.make_async_copy(corr_hbm, corr, load_sem.at[5])
+    small = [
+        pltpu.make_async_copy(source, place, load_sem.at[6 + k])
+        for k, (source, place) in enumerate(
+            (
+                (owner_hbm, owner), (block_nodes_hbm, block_nodes), (cell_nodes_hbm, cell_nodes),
+                (weights_hbm, weights), (shear_hbm, shear), (bulk_hbm, bulk), (target_hbm, target), (fixed_hbm, fixed),
+            )
+        )
+    ]
     load_now.start()
+    for load in small:
+        load.start()
     load_grads.start()
     load_prev.start()
     load_mass.start()
@@ -84,12 +96,14 @@
                 use(i, at, jnp.concatenate([wide[i : i + 1, 256 * r : 256 * r + 256] for r in range(8)], axis=0))
             return carry
 
-        lax.fori_loop(0, 16, move, 0)
+        lax.fori_loop(0, 16, move, 0, unroll=4)
 
     def set_state(i, at, value):
         state[i, at, :] = value
 
     load_now.wait()
+    for load in small:
+        load.wait()
     relaid(lines, set_state)
     for i in range(3):
         tables[1, 128 * i : 128 * i + 128, :] = state[i].astype(BF)
@@ -182,7 +196,7 @@
         nodes[quad] = jnp.concatenate(rows, axis=1)
         return carry
 
-    lax.fori_loop(0, 8, flatten, 0)
+    lax.fori_loop(0, 8, flatten, 0, unroll=4)
     rows_quad = lax.broadcasted_iota(jnp.int32, (128, QUAD), 0)
 
     def pick(total, row):
@@ -243,7 +257,7 @@
                 field[j, at, :] = jnp.dot(left, both, preferred_element_type=F32)
         return carry
 
-    lax.fori_loop(0, 8, gradient, 0, unroll=4)
+    lax.fori_loop(0, 8, gradient, 0, unroll=8)
     full = [
         [field[j, pl.ds(i, 32, stride=4), :] + (1.0 if i == j else 0.0) for j in range(3)]
         for i in range(3)
@@ -284,7 +298,7 @@
                 spread[quad, 128 * i : 128 * i + 128, span] = jnp.where(mask, value, 0.0).astype(BF)
         return carry
 
-    lax.fori_loop(0, 8, cell_forces, 0, unroll=4)
+    lax.fori_loop(0, 8, cell_forces, 0, unroll=8)
 
     def pair_copy(side):
         return pltpu.make_async_remote_copy(
@@ -476,9 +490,9 @@
         values[at, :] = jnp.dot(values[at, :].astype(BF), phi_bf[pair], preferred_element_type=F32)
         return carry
 
-    lax.fori_loop(0, 16, residual, 0, unroll=8)
-    lax.fori_loop(0, 16, correction, 0, unroll=8)
-    lax.fori_loop(0, 16, spreading, 0, unroll=8)
+    lax.fori_loop(0, 16, residual, 0, unroll=16)
+    lax.fori_loop(0, 16, correction, 0, unroll=16)
+    lax.fori_loop(0, 16, spreading, 0, unroll=16)
     gives = jnp.dot(to_slots, values[...].astype(BF), preferred_element_type=F32).astype(BF)
     giving[...] = gives.reshape(16, 16, 256)
     for q in FAR:
@@ -572,7 +586,7 @@
     block_owner, block_nodes, block_phi, block_corr, block_target, block_fixed,
 ):
     vmem = pl.BlockSpec(memory_space=pltpu.VMEM)
-    anywhere = pl.BlockSpec(memory_space=pl.ANY)
+    hbm = pl.BlockSpec(memory_space=pltpu.HBM)
     dma = pltpu.SemaphoreType.DMA
     message = pltpu.VMEM((16, 16, 256), BF)
     nodal = pltpu.VMEM((3, 8, 16, 256), BF)
@@ -581,9 +595,17 @@
         step_kernel,
         name="step",
         out_shape=jax.ShapeDtypeStruct((3, 128, 256), F32),
-        in_specs=[anywhere] * 3 + [vmem, anywhere] + [vmem] * 5 + [anywhere] * 2 + [vmem] * 2,
+        in_specs=[hbm] * 14,
         out_specs=vmem,
         scratch_shapes=[
+            pltpu.VMEM((32, 192), jnp.int32),
+            pltpu.VMEM((32, 128), F32),
+            pltpu.VMEM((1, 32), F32),
+            pltpu.VMEM((1, 32), F32),
+            pltpu.VMEM((1, 32), jnp.int32),
+            pltpu.VMEM((32, 256), jnp.int32),
+            pltpu.VMEM((3, 32, 128), F32),
+            pltpu.VMEM((32, 128), jnp.int32),
             pltpu.VMEM((3, 32768), F32),
             pltpu.VMEM((3, 32768), F32),
             pltpu.VMEM((256, 128), F32),
@@ -616,7 +638,7 @@
             pltpu.VMEM((128, 128), F32),
             pltpu.VMEM((384, 256), BF),
             pltpu.VMEM((16, 256, 1024), BF),
-            dma((6,)), pltpu.SemaphoreType.REGULAR, dma((3,)), dma((3,)), dma((3,)), dma((3,)), dma((11,)), dma((11,)),
+            dma((14,)), pltpu.SemaphoreType.REGULAR, dma((3,)), dma((3,)), dma((3,)), dma((3,)), dma((11,)), dma((11,)),
             dma((8,)), dma((8,)), dma((16,)), dma((16,)), dma((16,)), dma((16,)), dma((16,)), dma((16,)), dma((8,)),
             dma((8,)), dma((8,)), dma((8,)),
         ],

time: 77 us -> 72.8 us (0.945)
  Pallas kernels: 74.7 us -> 70.6 us
    pallas_call x1, Pallas kernels: 74.7 us -> 70.6 us  [body(): pl.pallas_call(step_kernel, name='step', out_shape=jax.ShapeDtypeStruct((...]
where the time goes in v5:
time: 72.8 us; the launch traced here: 72.7 us
  Pallas kernels  70.6 us (97%)
  local copies, waits for them, and re-layouts  2.06 us (3%)
    pallas_call x1, Pallas kernels, body(): pl.pallas_call(step_kernel, name='step', out_shape=jax.ShapeDtypeStruct((...  70.6 us
    unnamed x1, local copies, waits for them, and re-layouts  2.06 us

profile of v5, /device:TPU:1, one launch (start us, length us, event | category | flops | bytes accessed | tf_op | source)
XLA Modules:
  0.0 72.7 jit_solution(14361174846982994256)
XLA Ops:
  0.0 70.6 %step.1 = f32[3,128,256]{2,1,0:T(8,128)} custom-call(f32[3,32768]{1,0:T(4,128)} %now_hbm.1, f32[3,32768]{1,0:T(4,128)} %prev_hbm.1, f32[256,128]{1,0:T(8,128)} %bitcast.12, s32[32,192]{1,0:T(8,128)} %cell_nodes_hbm.1, bf16[32,3,192,128]{3,2,1,0:T(8,128)(2,1)} %grads_hbm.1, f32[32,128]{1,0:T(8,128)} %weights_hbm.1, f32[1,32]{1,0:T(1,128)} %bitcast.14, ...), custom_call_target="tpu_custom_call" | custom-call | tf_op jit(solution)/shard_map/step/pallas_call | solution.py:594
  70.6 2.1 %copy.15 = f32[1,3,128,256]{3,1,2,0:T(4,128)} copy(f32[1,3,128,256]{3,2,1,0:T(8,128)} %bitcast.11) | data formatting | bytes 786432

commit v6 on v5

--- a/solution.py
+++ b/solution.py
@@ -521,7 +521,7 @@
         adding[...] += total
         return carry
 
-    lax.fori_loop(0, 3, place_far, 0)
+    lax.fori_loop(0, 3, place_far, 0, unroll=3)
     for i in range(3):
         part[i] = adding[128 * i : 128 * i + 128, :].reshape(8, 16, 256).astype(BF)
 

time: 72.8 us -> 72.6 us (level)
  no operation moved by 1% of the time
where the time goes in v6:
time: 72.6 us; the launch traced here: 72.5 us
  Pallas kernels  70.4 us (97%)
  local copies, waits for them, and re-layouts  2.06 us (3%)
    pallas_call x1, Pallas kernels, body(): pl.pallas_call(step_kernel, name='step', out_shape=jax.ShapeDtypeStruct((...  70.4 us
    unnamed x1, local copies, waits for them, and re-layouts  2.06 us

profile of v6, /device:TPU:1, one launch (start us, length us, event | category | flops | bytes accessed | tf_op | source)
XLA Modules:
  0.0 72.5 jit_solution(7009941392912287518)
XLA Ops:
  0.0 70.4 %step.1 = f32[3,128,256]{2,1,0:T(8,128)} custom-call(f32[3,32768]{1,0:T(4,128)} %now_hbm.1, f32[3,32768]{1,0:T(4,128)} %prev_hbm.1, f32[256,128]{1,0:T(8,128)} %bitcast.12, s32[32,192]{1,0:T(8,128)} %cell_nodes_hbm.1, bf16[32,3,192,128]{3,2,1,0:T(8,128)(2,1)} %grads_hbm.1, f32[32,128]{1,0:T(8,128)} %weights_hbm.1, f32[1,32]{1,0:T(1,128)} %bitcast.14, ...), custom_call_target="tpu_custom_call" | custom-call | tf_op jit(solution)/shard_map/step/pallas_call | solution.py:594
  70.4 2.1 %copy.15 = f32[1,3,128,256]{3,1,2,0:T(4,128)} copy(f32[1,3,128,256]{3,2,1,0:T(8,128)} %bitcast.11) | data formatting | bytes 786432
